TPU v7x, 128 devices: a whole 4x4x4 slice. The times are simulated.
128 devices in a mesh: front: 8 (over z, core), helper: 16 (over x, y).
Axes of the slice: x: 4, y: 4, z: 4, core: 2. Of those that a mesh axis runs over, the one named last changes fastest.
Arguments:
- front: float32 [8, 4096, 4096], P('front', 'helper')
- row_list: int32 [8, 4096], replicated, may hold values from 0 to 4095, as said below
- child_map: int32 [8, 3840], replicated, may hold values from 0 to 8191, as said below
- parent: float32 [8192, 8192], P(('front', 'helper')), may hold values from -6 to 6
Outputs:
- factors: float32 [8, 4096, 4096], P('front', 'helper')
- assembled: float32 [8192, 8192], P(('front', 'helper'))
Inputs may be any that keep to these rules, and one draw needn't show every extreme that they name: Each row of row_list is a permutation; stored rows h * 256 to (h + 1) * 256 - 1 of a front lie on helper h. Of the 256 rows of any panel, one helper holds at most 24, and some helper holds exactly 24 in every panel. The leading 256 x 256 block of every front is well conditioned without pivoting: its diagonal exceeds 2.5 sqrt(256) times the row's spread. `child_map`: distinct within a front. Parent row r lies on device r // 64 of front+helper. Of the contribution rows on one device, at most 2 go to one device's parent rows, and exactly 2 go to some device.
All inputs are finite; a program needn't handle non-finite values.
Results may differ from a plain program's by a relative error of at most 0.0001.
Values sent between devices are 32-bit elements; how exact they have to be, the bound alone decides.
No kernel may reach another device: no remote copies, remote signals or barrier semaphores. Data moves between devices by JAX's collectives and lax.ppermute only.
A program may use at most 128 MiB of HBM per device.

v0:
```python
import jax
import jax.numpy as jnp
from jax import lax
from jax.sharding import PartitionSpec as P

PANEL = 256
PIVOTS = 256


def product(left, right):
    return jnp.dot(left, right, precision=lax.Precision.HIGHEST, preferred_element_type=jnp.float32)


def small_inverse(matrix):
    extent = matrix.shape[0]
    augmented = jnp.concatenate([matrix, jnp.eye(extent, dtype=matrix.dtype)], axis=1)
    for column in range(extent):
        pivot_row = augmented[column] / augmented[column, column]
        augmented = augmented - augmented[:, column : column + 1] * pivot_row[None, :]
        augmented = augmented.at[column].set(pivot_row)
    return augmented[:, extent:]


def block_inverse(matrix):
    extent = matrix.shape[0]
    if extent <= 32:
        return small_inverse(matrix)
    middle = extent // 2
    upper_left = matrix[:middle, :middle]
    upper_right = matrix[:middle, middle:]
    lower_left = matrix[middle:, :middle]
    lower_right = matrix[middle:, middle:]
    inverse_left = block_inverse(upper_left)
    coupled = product(inverse_left, upper_right)
    schur_part = lower_right - product(lower_left, coupled)
    inverse_schur = block_inverse(schur_part)
    left_factor = product(lower_left, inverse_left)
    top_right = -product(coupled, inverse_schur)
    bottom_left = -product(inverse_schur, left_factor)
    top_left = inverse_left - product(top_right, left_factor)
    upper_half = jnp.concatenate([top_left, top_right], axis=1)
    lower_half = jnp.concatenate([bottom_left, inverse_schur], axis=1)
    return jnp.concatenate([upper_half, lower_half], axis=0)


def local(front, row_list, child_map, parent):
    front_rows = front[0]
    row_count = front_rows.shape[0]
    helpers = lax.axis_size("helper")
    fronts = lax.axis_size("front")
    devices_all = helpers * fronts
    my_front = lax.axis_index("front")
    my_helper = lax.axis_index("helper")
    front_order = jnp.take(row_list, my_front, axis=0)
    own_ids = lax.dynamic_slice_in_dim(front_order, my_helper * row_count, row_count)
    local_iota = jnp.arange(row_count, dtype=jnp.int32)
    panel_iota = jnp.arange(PANEL, dtype=jnp.int32)
    end_col = PANEL
    trailing = front_rows
    wanted = own_ids[None, :] == (0 + panel_iota)[:, None]
    position = jnp.sum(jnp.where(wanted, local_iota[None, :], 0), axis=1)
    present = jnp.any(wanted, axis=1)
    picked = jnp.where(present[:, None], jnp.take(trailing, position, axis=0), 0.0)
    panel_rows = lax.psum(picked, "helper")
    inverse = block_inverse(panel_rows[:, :PANEL])
    active = (own_ids >= end_col)[:, None]
    current = front_rows[:, 0:end_col]
    lower_part = jnp.where(active, product(current, inverse), 0.0)
    front_rows = front_rows.at[:, 0:end_col].set(jnp.where(active, lower_part, current))
    front_rows = front_rows.at[:, end_col:].add(-product(lower_part, panel_rows[:, PANEL:]))
    parent_rows = parent.shape[0]
    parent_width = parent.shape[1]
    cb_width = front_rows.shape[1] - PIVOTS
    cap_rows = (row_count + devices_all - 1) // devices_all
    device_iota = jnp.arange(devices_all, dtype=jnp.int32)
    own_map = jnp.take(child_map, my_front, axis=0)
    own_cb = own_ids >= PIVOTS
    own_target = jnp.take(own_map, jnp.clip(own_ids - PIVOTS, 0, cb_width - 1))
    owner = jnp.where(own_cb, own_target // parent_rows, devices_all)
    dest_match = owner[:, None] == device_iota[None, :]
    dest_rank = jnp.sum(
        jnp.where(dest_match, jnp.cumsum(dest_match.astype(jnp.int32), axis=0) - 1, 0), axis=1
    )
    outgoing = jnp.zeros((devices_all, cap_rows, cb_width), jnp.float32)
    outgoing = outgoing.at[owner, dest_rank].set(front_rows[:, PIVOTS:], mode="drop")
    received = lax.all_to_all(
        outgoing, ("front", "helper"), split_axis=0, concat_axis=0, tiled=True
    )
    me_flat = my_front * helpers + my_helper
    all_cb = row_list >= PIVOTS
    all_target = jnp.take_along_axis(
        child_map, jnp.clip(row_list - PIVOTS, 0, cb_width - 1), axis=1
    )
    to_me = (all_cb & (all_target // parent_rows == me_flat)).reshape(devices_all, row_count)
    arrive_rank = jnp.cumsum(to_me.astype(jnp.int32), axis=1) - 1
    arrive_slot = jnp.where(to_me, arrive_rank, cap_rows)
    source_iota = jnp.broadcast_to(device_iota[:, None], (devices_all, row_count))
    local_target = (all_target % parent_rows).reshape(devices_all, row_count)
    dest_row = jnp.full((devices_all, cap_rows), parent_rows, jnp.int32)
    dest_row = dest_row.at[source_iota, arrive_slot].set(local_target, mode="drop")
    front_received = received.reshape(fronts, helpers * cap_rows, cb_width)
    front_dest = dest_row.reshape(fronts, helpers * cap_rows)
    front_iota = jnp.arange(fronts, dtype=jnp.int32)
    column_iota = jnp.arange(cb_width, dtype=jnp.int32)
    column_slot = jnp.full((fronts, parent_width), cb_width, jnp.int32)
    column_slot = column_slot.at[front_iota[:, None], child_map].set(
        jnp.broadcast_to(column_iota[None, :], (fronts, cb_width))
    )
    assembled = parent
    for front_index in range(fronts):
        local_block = jnp.zeros((parent_rows, cb_width), jnp.float32)
        local_block = local_block.at[front_dest[front_index]].add(
            front_received[front_index], mode="drop"
        )
        slot_row = column_slot[front_index]
        spread = jnp.take(local_block, jnp.minimum(slot_row, cb_width - 1), axis=1)
        assembled = assembled + jnp.where((slot_row < cb_width)[None, :], spread, 0.0)
    return (front_rows[None], assembled)


def solution(mesh):
    in_specs = (P("front", "helper", None), P(), P(), P(("front", "helper"), None))
    out_specs = (P("front", "helper", None), P(("front", "helper"), None))
    return jax.shard_map(local, mesh=mesh, in_specs=in_specs, out_specs=out_specs, check_vma=False)
```

profile of v0, /device:TPU:1, one launch (start us, length us, event | category | flops | bytes accessed | tf_op | source)
XLA Modules:
  0.0 1454.7 jit_solution(10219497662299477515)
XLA Ops:
  8.3 7.9 gather_fusion
  16.2 5.1 select_select_fusion
  24.3 5.6 copy.76
  30.1 198.6 %gather_fusion.2 = s32[32768]{0:T(1024)S(1)} fusion(s32[8,3840]{1,0:T(8,128)S(1)} %copy-done, s32[32768]{0:T(1024)S(1)} %bitcast.916), kind=kCustom, calls=%fused_computation.10 | custom fusion | bytes 524288 | tf_op jit(solution)/shard_map/jit(take_along_axis)/gather | solution.py:91
  228.9 4.4 copy.373
  809.9 2.4 fusion.27
  812.3 2.3 copy.374
  817.0 8.8 bitcast_dynamic-update-slice_fusion
  825.8 2.0 copy-done.2
  827.8 5.5 copy.89
  833.3 2.9 broadcast_in_dim.200
  836.2 49.8 %scatter_fusion = f32[128,2,3840]{2,1,0:T(2,128)} fusion(f32[128,2,3840]{2,1,0:T(2,128)} %broadcast_in_dim.200, s32[256]{0:T(256)S(1)} %bitcast.921, f32[256,3840]{1,0:T(8,128)} %copy.89), kind=kCustom, calls=%fused_computation.11 | custom fusion | bytes 11798528 | tf_op jit(solution)/shard_map/scatter | solution.py:85
  886.0 11.8 all-to-all-start
  899.2 120.0 %scatter_custom_fusion.10 = s32[256]{0:T(256)S(1)} fusion(s32[32768]{0:T(1024)S(1)} %bitcast.924, s32[32768]{0:T(1024)S(1)} %bitcast.923, s32[]{:T(128)} %constant.5596.clone.1), kind=kCustom, calls=%fused_computation.1055 | custom fusion | bytes 1028
  1020.8 2.7 copy.91
  1023.5 112.6 %scatter_custom_fusion.9 = s32[65536]{0:T(1024)S(1)} fusion(s32[30720]{0:T(1024)S(1)} %reshape.6392, s32[30720]{0:T(1024)S(1)} %reshape.6394, s32[]{:T(128)} %constant.5549.clone.1), kind=kCustom, calls=%fused_computation.141 | custom fusion | bytes 262148
  1139.9 5.6 copy.106
  1145.5 3.2 fusion.158
  1148.7 2.2 reshape.6332
  1159.3 1.9 scatter_custom_fusion.3
  1163.1 2.2 scatter_custom_fusion.4
  1170.9 1.9 scatter_custom_fusion.6
  1185.8 29.3 %gather_fusion.3 = f32[8192,64]{1,0:T(8,128)} fusion(f32[64,3840]{0,1:T(8,128)} %copy.90, s32[8192]{0:T(1024)S(1)} %copy-done.10), kind=kCustom, calls=%fused_computation.clone | custom fusion | bytes 4227072 | tf_op jit(solution)/shard_map/jit(_take)/gather | solution.py:116
  1215.1 29.3 %gather_fusion.10 = f32[8192,64]{1,0:T(8,128)} fusion(f32[64,3840]{0,1:T(8,128)} %copy.105, s32[8192]{0:T(1024)S(1)} %copy-done.9), kind=kCustom, calls=%fused_computation.7.clone | custom fusion | bytes 4227072 | tf_op jit(solution)/shard_map/jit(_take)/gather | solution.py:116
  1244.4 29.2 %gather_fusion.9 = f32[8192,64]{1,0:T(8,128)} fusion(f32[64,3840]{0,1:T(8,128)} %copy.103, s32[8192]{0:T(1024)S(1)} %copy-done.8), kind=kCustom, calls=%fused_computation.6.clone | custom fusion | bytes 4227072 | tf_op jit(solution)/shard_map/jit(_take)/gather | solution.py:116
  1273.6 29.2 %gather_fusion.8 = f32[8192,64]{1,0:T(8,128)} fusion(f32[64,3840]{0,1:T(8,128)} %copy.101, s32[8192]{0:T(1024)S(1)} %copy-done.7), kind=kCustom, calls=%fused_computation.5.clone | custom fusion | bytes 4227072 | tf_op jit(solution)/shard_map/jit(_take)/gather | solution.py:116
  1302.8 29.3 %gather_fusion.7 = f32[8192,64]{1,0:T(8,128)} fusion(f32[64,3840]{0,1:T(8,128)} %copy.99, s32[8192]{0:T(1024)S(1)} %copy-done.6), kind=kCustom, calls=%fused_computation.4.clone | custom fusion | bytes 4227072 | tf_op jit(solution)/shard_map/jit(_take)/gather | solution.py:116
  1332.1 29.3 %gather_fusion.6 = f32[8192,64]{1,0:T(8,128)} fusion(f32[64,3840]{0,1:T(8,128)} %copy.97, s32[8192]{0:T(1024)S(1)} %get-tuple-element.3164), kind=kCustom, calls=%fused_computation.3.clone | custom fusion | bytes 4227072 | tf_op jit(solution)/shard_map/jit(_take)/gather | solution.py:116
  1361.4 29.2 %gather_fusion.5 = f32[8192,64]{1,0:T(8,128)} fusion(f32[64,3840]{0,1:T(8,128)} %copy.95, s32[8192]{0:T(1024)S(1)} %get-tuple-element.3165), kind=kCustom, calls=%fused_computation.2.clone | custom fusion | bytes 4227072 | tf_op jit(solution)/shard_map/jit(_take)/gather | solution.py:116
  1390.7 27.7 %gather_fusion.4 = f32[8192,64]{1,0:T(8,128)} fusion(f32[64,3840]{0,1:T(8,128)S(1)} %copy.93, s32[8192]{0:T(1024)S(1)} %get-tuple-element.3166), kind=kCustom, calls=%fused_computation.1.clone | custom fusion | bytes 4227072 | tf_op jit(solution)/shard_map/jit(_take)/gather | solution.py:116
  1418.5 25.1 %fusion.1 = f32[64,8192]{0,1:T(8,128)} fusion(f32[64,8192]{0,1:T(8,128)} %copy.91, f32[8192,64]{1,0:T(8,128)} %gather_fusion.10, f32[8192,64]{1,0:T(8,128)} %gather_fusion.9, f32[8192,64]{1,0:T(8,128)} %gather_fusion.8, f32[8192,64]{1,0:T(8,128)} %gather_fusion.7, f32[8192,64]{1,0:T(8,128)} %gather_fusion.6, f32[8192,64]{1,0:T(8,128)} %gather_fusion.5, ...), kind=kLoop, calls=%fused_computation.25 | loop fusion | flops 12582912 | bytes 21102592 | tf_op jit(solution)/shard_map/add | solution.py:117
  1443.6 3.8 copy.107
  (1738 shorter events, 614.1 us)
Async XLA Ops:
  7.2 227.4 %all-reduce.2.cloned.1.call-start = ((), (), s32[]{:S(2)}) async-start(), calls=%async_computation.1 | async-start | bytes 8388608 | tf_op jit(solution)/shard_map/psum | solution.py:64
  21.2 0.9 copy-start
  24.3 5.8 copy-start.5
  228.9 5.4 copy-start.28
  228.9 5.4 copy-start.27
  812.3 3.4 copy-start.1
  812.3 4.7 copy-start.3
  825.8 2.0 copy-start.2
  886.0 12.9 copy-start.26
  886.0 13.0 copy-start.25
  886.0 259.5 %all-to-all-start = ((f32[128,2,3840]{2,1,0:T(2,128)}), f32[128,2,3840]{2,1,0:T(2,128)}, u32[]{:S(2)}, u32[]{:S(2)}) async-start(f32[128,2,3840]{2,1,0:T(2,128)} %scatter_fusion), calls=%async_computation | async-start | bytes 7864320 | tf_op jit(solution)/shard_map/all_to_all | solution.py:86
  897.8 123.0 %copy-start.4 = (f32[64,8192]{1,0:T(8,128)S(1)}, f32[64,8192]{1,0:T(8,128)}, u32[]{:S(2)}) copy-start(f32[64,8192]{1,0:T(8,128)} %param.525) | copy-start | bytes 6291460
  1178.2 7.6 copy-start.10
  1185.8 29.3 %copy-start.9 = (s32[8192]{0:T(1024)S(1)}, s32[8192]{0:T(1024)}, u32[]{:S(2)}) copy-start(s32[8192]{0:T(1024)} %get-tuple-element.3167) | copy-start | bytes 98308
  1215.1 29.3 %copy-start.8 = (s32[8192]{0:T(1024)S(1)}, s32[8192]{0:T(1024)}, u32[]{:S(2)}) copy-start(s32[8192]{0:T(1024)} %get-tuple-element.3161) | copy-start | bytes 98308
  1244.4 29.3 %copy-start.7 = (s32[8192]{0:T(1024)S(1)}, s32[8192]{0:T(1024)}, u32[]{:S(2)}) copy-start(s32[8192]{0:T(1024)} %get-tuple-element.3162) | copy-start | bytes 98308
  1273.6 29.2 %copy-start.6 = (s32[8192]{0:T(1024)S(1)}, s32[8192]{0:T(1024)}, u32[]{:S(2)}) copy-start(s32[8192]{0:T(1024)} %get-tuple-element.3163) | copy-start | bytes 98308
  1390.6 27.8 %copy-start.11 = (pred[8192]{0:T(1024)(128)(4,1)S(1)}, pred[8192]{0:T(1024)(128)(4,1)}, u32[]{:S(2)}) copy-start(pred[8192]{0:T(1024)(128)(4,1)} %get-tuple-element.3146) | copy-start | bytes 24580
  1390.6 27.8 %copy-start.12 = (pred[8192]{0:T(1024)(128)(4,1)S(1)}, pred[8192]{0:T(1024)(128)(4,1)}, u32[]{:S(2)}) copy-start(pred[8192]{0:T(1024)(128)(4,1)} %get-tuple-element.3147) | copy-start | bytes 24580
  1390.6 27.8 %copy-start.13 = (pred[8192]{0:T(1024)(128)(4,1)S(1)}, pred[8192]{0:T(1024)(128)(4,1)}, u32[]{:S(2)}) copy-start(pred[8192]{0:T(1024)(128)(4,1)} %get-tuple-element.3148) | copy-start | bytes 24580
  1390.6 27.8 %copy-start.14 = (pred[8192]{0:T(1024)(128)(4,1)S(1)}, pred[8192]{0:T(1024)(128)(4,1)}, u32[]{:S(2)}) copy-start(pred[8192]{0:T(1024)(128)(4,1)} %get-tuple-element.3149) | copy-start | bytes 24580
  1390.6 27.8 %copy-start.15 = (pred[8192]{0:T(1024)(128)(4,1)S(1)}, pred[8192]{0:T(1024)(128)(4,1)}, u32[]{:S(2)}) copy-start(pred[8192]{0:T(1024)(128)(4,1)} %get-tuple-element.3150) | copy-start | bytes 24580
  1390.6 27.8 %copy-start.16 = (pred[8192]{0:T(1024)(128)(4,1)S(1)}, pred[8192]{0:T(1024)(128)(4,1)}, u32[]{:S(2)}) copy-start(pred[8192]{0:T(1024)(128)(4,1)} %get-tuple-element.3151) | copy-start | bytes 24580
  1390.6 27.8 %copy-start.17 = (pred[8192]{0:T(1024)(128)(4,1)S(1)}, pred[8192]{0:T(1024)(128)(4,1)}, u32[]{:S(2)}) copy-start(pred[8192]{0:T(1024)(128)(4,1)} %get-tuple-element.3152) | copy-start | bytes 24580
  1390.6 27.8 %copy-start.18 = (pred[8192]{0:T(1024)(128)(4,1)S(1)}, pred[8192]{0:T(1024)(128)(4,1)}, u32[]{:S(2)}) copy-start(pred[8192]{0:T(1024)(128)(4,1)} %get-tuple-element.3153) | copy-start | bytes 24580
  1390.7 27.8 %copy-start.19 = (pred[8192]{0:T(1024)(128)(4,1)S(1)}, pred[8192]{0:T(1024)(128)(4,1)}, u32[]{:S(2)}) copy-start(pred[8192]{0:T(1024)(128)(4,1)} %get-tuple-element.3154) | copy-start | bytes 24580
  1390.7 27.8 %copy-start.20 = (pred[8192]{0:T(1024)(128)(4,1)S(1)}, pred[8192]{0:T(1024)(128)(4,1)}, u32[]{:S(2)}) copy-start(pred[8192]{0:T(1024)(128)(4,1)} %get-tuple-element.3155) | copy-start | bytes 24580
  1390.7 27.8 %copy-start.21 = (pred[8192]{0:T(1024)(128)(4,1)S(1)}, pred[8192]{0:T(1024)(128)(4,1)}, u32[]{:S(2)}) copy-start(pred[8192]{0:T(1024)(128)(4,1)} %get-tuple-element.3156) | copy-start | bytes 24580
  1390.7 27.8 %copy-start.22 = (pred[8192]{0:T(1024)(128)(4,1)S(1)}, pred[8192]{0:T(1024)(128)(4,1)}, u32[]{:S(2)}) copy-start(pred[8192]{0:T(1024)(128)(4,1)} %get-tuple-element.3157) | copy-start | bytes 24580
  1390.7 27.8 %copy-start.23 = (pred[8192]{0:T(1024)(128)(4,1)S(1)}, pred[8192]{0:T(1024)(128)(4,1)}, u32[]{:S(2)}) copy-start(pred[8192]{0:T(1024)(128)(4,1)} %get-tuple-element.3158) | copy-start | bytes 24580
  1390.7 27.8 %copy-start.24 = (pred[8192]{0:T(1024)(128)(4,1)S(1)}, pred[8192]{0:T(1024)(128)(4,1)}, u32[]{:S(2)}) copy-start(pred[8192]{0:T(1024)(128)(4,1)} %get-tuple-element.3159) | copy-start | bytes 24580
Sparse Core Ops, SparseCore 0:
  21.4 106.3 all-reduce.1
where the time goes:
time: 1470 us; the launch traced here: 1450 us
  local copies, waits for them, and re-layouts  995 us (68%)
  other arithmetic  402 us (27%)
  matrix products  26.1 us (2%)
  between operations  19.8 us (1%)
    unnamed x70, local copies, waits for them, and re-layouts  263 us
    gather x8, local copies, waits for them, and re-layouts, local(): spread = jnp.take(local_block, jnp.minimum(slot_row, cb_width - 1), axis=1)  232 us
    gather x2, local copies, waits for them, and re-layouts, local(): jnp.take_along_axis(child_map, jnp.clip(row_list - PIVOTS, 0, cb_width -...  199 us
    div x256, other arithmetic, small_inverse(): pivot_row = augmented[column] / augmented[column, column]  167 us
    mul x248, other arithmetic, small_inverse(): augmented = augmented - augmented[:, column:column + 1] * pivot_row[None, :]  161 us
    slice x256, local copies, waits for them, and re-layouts, small_inverse(): pivot_row = augmented[column] / augmented[column, column]  151 us
    scatter x1, local copies, waits for them, and re-layouts, local(): outgoing.at[owner, dest_rank].set(front_rows[:, PIVOTS:], mode='drop')  49.8 us
    slice x256, local copies, waits for them, and re-layouts, small_inverse(): augmented = augmented - augmented[:, column:column + 1] * pivot_row[None, :]  45.7 us
  transfers between devices with their start and end apart: 2, of which 0 were waited for; matrix products, arithmetic and copies ran while one was open for 32% of the time, Pallas kernels for 0%

commit v1 on v0

v1 whole, which is shorter than its diff:
```python
import jax
import jax.numpy as jnp
from jax import lax
from jax.experimental import pallas as pl
from jax.experimental.pallas import tpu as pltpu
from jax.sharding import PartitionSpec as P

PIVOTS = 256
CAP = 24
BASE = 32
F32 = jnp.float32
BF16 = jnp.bfloat16
I32 = jnp.int32
GRID = 4
X_UP, X_DOWN, Y_UP, Y_DOWN = (1, 0), (3, 0), (0, 1), (0, 3)
BIG = pltpu.CompilerParams(vmem_limit_bytes=58 << 20)


def iota(shape, axis):
    return lax.broadcasted_iota(I32, shape, axis)


def exact(left, right):
    return jnp.dot(left, right, precision=lax.Precision.HIGHEST, preferred_element_type=F32)


def halves(value):
    high = value.astype(BF16)
    return high, (value - high.astype(F32)).astype(BF16)


def dot16(left, right):
    return jnp.dot(left, right, preferred_element_type=F32)


def dot3(left, right):
    left_high, left_low = halves(left)
    right_high, right_low = halves(right)
    return dot16(left_high, right_high) + (dot16(left_high, right_low) + dot16(left_low, right_high))


def select_kernel(ids_ref, front_ref, pivot_ref, first_ref, second_ref):
    rows = front_ref.shape[0]
    half = first_ref.shape[1]
    ids = ids_ref[...]
    inside = jnp.broadcast_to((ids < PIVOTS).astype(F32), (8, rows)).astype(BF16)
    before = (iota((rows, rows), 0) < iota((rows, rows), 1)).astype(F32).astype(BF16)
    rank = dot16(inside, before)[:1].astype(I32)
    rank = jnp.where(ids < PIVOTS, rank, -1)
    chosen = (jnp.broadcast_to(rank, (CAP, rows)) == iota((CAP, rows), 0)).astype(F32)
    pivot_ref[...] = exact(chosen, front_ref[:, :PIVOTS])
    step = 384
    for start in range(0, half, step):
        first_ref[:, start : start + step] = exact(chosen, front_ref[:, PIVOTS + start : PIVOTS + start + step])
        at = PIVOTS + half + start
        second_ref[:, start : start + step] = exact(chosen, front_ref[:, at : at + step])


def select_panel(own_ids, front_rows):
    half = (front_rows.shape[1] - PIVOTS) // 2
    return pl.pallas_call(
        select_kernel,
        out_shape=(
            jax.ShapeDtypeStruct((CAP, PIVOTS), F32),
            jax.ShapeDtypeStruct((CAP, half), F32),
            jax.ShapeDtypeStruct((CAP, half), F32),
        ),
        compiler_params=BIG,
    )(own_ids[None, :], front_rows)


def shift_pairs(step):
    return [
        (x * GRID + y, (x + step[0]) % GRID * GRID + (y + step[1]) % GRID)
        for x in range(GRID)
        for y in range(GRID)
    ]


def shift(value, step):
    return lax.ppermute(value, "helper", shift_pairs(step))


def spread_panel(first, second):
    cut = 16
    first_up, first_down = shift(first, X_UP), shift(first, X_DOWN)
    second_up, second_down = shift(second, Y_UP), shift(second, Y_DOWN)
    first_far = shift(first_up[:cut], X_UP), shift(first_down[cut:], X_DOWN)
    second_far = shift(second_up[:cut], Y_UP), shift(second_down[cut:], Y_DOWN)
    line = jnp.concatenate([first, first_up, first_down, *first_far])
    file = jnp.concatenate([second, second_up, second_down, *second_far])
    middle = 2 * CAP
    line_up, line_down = shift(line, Y_UP), shift(line, Y_DOWN)
    file_up, file_down = shift(file, X_UP), shift(file, X_DOWN)
    line_far = shift(line_up[:middle], Y_UP), shift(line_down[middle:], Y_DOWN)
    file_far = shift(file_up[:middle], X_UP), shift(file_down[middle:], X_DOWN)
    return (line, line_up, line_down, *line_far), (file, file_up, file_down, *file_far)


def inverse_kernel(slot_abs_ref, slot_rel_ref, piv_ref, inv_ref, inv_rel_ref):
    slots = piv_ref.shape[0]
    natural = (iota((PIVOTS, slots), 0) == slot_abs_ref[...]).astype(F32)
    inv_ref[...] = exact(natural, piv_ref[...])
    lanes = iota((1, PIVOTS), 1)
    for block in range(PIVOTS // BASE):
        base = block * BASE
        rows = inv_ref[base : base + BASE, :]
        sub = iota((BASE, 1), 0)
        for step in range(BASE):
            at = base + step
            here = lanes == at
            pivot_row = rows[step : step + 1, :]
            scaled = jnp.where(here, 1.0, pivot_row) / pivot_row[:, at : at + 1]
            column = rows[:, at : at + 1]
            rows = jnp.where(sub == step, scaled, jnp.where(here, 0.0, rows) - column * scaled)
        in_block = (lanes >= base) & (lanes < base + BASE)
        full = inv_ref[...]
        left = jnp.where(in_block, full, 0.0)
        kept = jnp.where(in_block, 0.0, full)
        parts = []
        if base:
            parts.append(jnp.zeros((base, PIVOTS), F32))
        parts.append(rows)
        if base + BASE < PIVOTS:
            parts.append(jnp.zeros((PIVOTS - base - BASE, PIVOTS), F32))
        inv_ref[...] = kept - exact(left, jnp.concatenate(parts, axis=0))
        inv_ref[base : base + BASE, :] = rows
    relative = (iota((PIVOTS, slots), 0) == slot_rel_ref[...]).astype(F32)
    inv_rel_ref[...] = exact(inv_ref[...], relative)


def invert(slot_abs, slot_rel, piv):
    slots = piv.shape[0]
    return pl.pallas_call(
        inverse_kernel,
        out_shape=(
            jax.ShapeDtypeStruct((PIVOTS, PIVOTS), F32),
            jax.ShapeDtypeStruct((PIVOTS, slots), F32),
        ),
        compiler_params=BIG,
    )(slot_abs, slot_rel, piv)


OFFSETS = (0, 3, 1, 2)


def eliminate_kernel(
    active_ref, place_ref, rank_ref, inv_ref, inv_rel_ref, front_ref, *refs
):
    first_refs, second_refs = refs[:5], refs[5:10]
    factors_ref, send_ref, upper, sorted_in = refs[10:]
    rows = front_ref.shape[0]
    width = front_ref.shape[1] - PIVOTS
    half = width // 2
    for piece in range(4):
        for block in range(4):
            into = (block * 4 + piece) * CAP
            if piece < 3:
                upper[into : into + CAP, :half] = first_refs[piece][block * CAP : (block + 1) * CAP, :]
            else:
                at = block % 2 * CAP
                upper[into : into + CAP, :half] = first_refs[3 + block // 2][at : at + CAP, :]
            into = (piece * 4 + block) * CAP
            if piece < 3:
                upper[into : into + CAP, half:] = second_refs[piece][block * CAP : (block + 1) * CAP, :]
            else:
                at = block % 2 * CAP
                upper[into : into + CAP, half:] = second_refs[3 + block // 2][at : at + CAP, :]
    active = active_ref[...] > 0
    current = front_ref[:, :PIVOTS]
    factors_ref[:, :PIVOTS] = jnp.where(active, dot3(current, inv_ref[...]), current)
    lower = jnp.where(active, dot3(current, inv_rel_ref[...]), 0.0)
    lower_high, lower_low = halves(lower)
    place = (iota((rows, rows), 0) == place_ref[...]).astype(F32).astype(BF16)
    tile = 256

    def update(index, carry):
        at = pl.multiple_of(index * tile, tile)
        high, low = halves(upper[:, pl.ds(at, tile)])
        change = dot16(lower_high, high) + (dot16(lower_high, low) + dot16(lower_low, high))
        out = front_ref[:, pl.ds(at + PIVOTS, tile)] - change
        factors_ref[:, pl.ds(at + PIVOTS, tile)] = out
        high, low = halves(out)
        sorted_in[:rows, pl.ds(at, tile)] = dot16(place, high).astype(BF16)
        sorted_in[rows:, pl.ds(at, tile)] = dot16(place, low).astype(BF16)
        return carry

    lax.fori_loop(0, width // tile, update, 0)

    def permute(index, carry):
        at = pl.multiple_of(index * tile, tile)
        lane = iota((1, 128), 1) + at
        ranks = rank_ref[...]
        moves = jnp.concatenate([(ranks == lane), (ranks == lane + 128)], axis=1).astype(F32).astype(BF16)
        out = dot16(sorted_in[...], moves)
        send_ref[:, pl.ds(at, tile)] = out[:rows] + out[rows:]
        return carry

    lax.fori_loop(0, width // tile, permute, 0)


def eliminate(active, place, rank, inv, inv_rel, front_rows, line, file):
    rows, columns = front_rows.shape
    width = columns - PIVOTS
    return pl.pallas_call(
        eliminate_kernel,
        out_shape=(
            jax.ShapeDtypeStruct((rows, columns), F32),
            jax.ShapeDtypeStruct((rows, width), F32),
        ),
        scratch_shapes=[
            pltpu.VMEM((16 * CAP, width), F32),
            pltpu.VMEM((2 * rows, width), BF16),
        ],
        compiler_params=BIG,
    )(active, place, rank, inv, inv_rel, front_rows, *line, *file)


def assemble_kernel(group_ref, source_ref, put_ref, received_ref, parent_ref, out_ref):
    fronts = source_ref.shape[0]
    per_front = received_ref.shape[0] // fronts
    last = received_ref.shape[1] // 128 - 1
    step = pl.program_id(0)
    tile = out_ref.shape[1]
    columns = []
    for part in range(tile // 128):
        pieces = []
        for front in range(fronts):
            group = jnp.minimum(group_ref[front, step * (tile // 128) + part], last)
            following = jnp.minimum(group + 1, last)
            source = source_ref[front : front + 1, part * 128 : (part + 1) * 128]
            lane = jnp.broadcast_to(source & 127, (per_front, 128))
            which = source >> 7
            span = pl.ds(front * per_front, per_front)
            near = received_ref[span, pl.ds(pl.multiple_of(group * 128, 128), 128)]
            far = received_ref[span, pl.ds(pl.multiple_of(following * 128, 128), 128)]
            near = jnp.take_along_axis(near, lane, axis=1)
            far = jnp.take_along_axis(far, lane, axis=1)
            pieces.append(jnp.where(which == group, near, jnp.where(which == following, far, 0.0)))
        columns.append(jnp.concatenate(pieces, axis=0))
    spread = jnp.concatenate(columns, axis=1)
    high, low = halves(spread)
    put = put_ref[...]
    out_ref[...] = parent_ref[...] + (dot16(put, high) + dot16(put, low))


def assemble(group, source, put, received, parent):
    rows, width = parent.shape
    fronts = source.shape[0]
    tile = 256
    return pl.pallas_call(
        assemble_kernel,
        grid_spec=pltpu.PrefetchScalarGridSpec(
            num_scalar_prefetch=1,
            grid=(width // tile,),
            in_specs=[
                pl.BlockSpec((fronts, tile), lambda i, g: (0, i)),
                pl.BlockSpec(put.shape, lambda i, g: (0, 0)),
                pl.BlockSpec(received.shape, lambda i, g: (0, 0)),
                pl.BlockSpec((rows, tile), lambda i, g: (0, i)),
            ],
            out_specs=pl.BlockSpec((rows, tile), lambda i, g: (0, i)),
        ),
        out_shape=jax.ShapeDtypeStruct((rows, width), F32),
        compiler_params=BIG,
    )(group, source, put, received, parent)


def local(front, row_list, child_map, parent):
    front_rows = front[0]
    rows = front_rows.shape[0]
    width = front_rows.shape[1] - PIVOTS
    helpers = lax.axis_size("helper")
    fronts = lax.axis_size("front")
    devices = helpers * fronts
    cap = (rows + devices - 1) // devices
    parent_rows, parent_width = parent.shape
    my_front = lax.axis_index("front")
    my_helper = lax.axis_index("helper")
    me = my_front * helpers + my_helper
    order = jnp.take(row_list, my_front, axis=0)
    by_helper = order.reshape(helpers, rows)
    own_ids = lax.dynamic_slice_in_dim(order, my_helper * rows, rows)

    pivot, first, second = select_panel(own_ids, front_rows)
    piv = lax.all_gather(pivot, "helper", axis=0, tiled=True)
    line, file = spread_panel(first, second)

    inside = by_helper < PIVOTS
    earlier = (jnp.arange(rows)[:, None] < jnp.arange(rows)[None, :]).astype(BF16)
    slot_rank = dot16(inside.astype(BF16), earlier).astype(I32)
    slot_iota = jnp.arange(CAP, dtype=I32)
    hit = (slot_rank[:, None, :] == slot_iota[None, :, None]) & inside[:, None, :]
    slot_row = jnp.sum(jnp.where(hit, by_helper[:, None, :] + 1, 0), axis=2) - 1
    grid_iota = jnp.array(OFFSETS, I32)
    source_x = (my_helper // GRID + grid_iota) % GRID
    source_y = (my_helper % GRID + grid_iota) % GRID
    relative = (source_x[:, None] * GRID + source_y[None, :]).reshape(helpers)
    slot_rel = jnp.sum(
        jnp.where((relative[:, None] == jnp.arange(helpers)[None, :])[:, :, None], slot_row[None], 0), axis=1
    )
    inv, inv_rel = invert(slot_row.reshape(1, -1), slot_rel.reshape(1, -1), piv)

    own_map = jnp.take(child_map, my_front, axis=0)
    own_cb = own_ids >= PIVOTS
    column_iota = jnp.arange(width, dtype=I32)
    own_target = jnp.sum(
        jnp.where((own_ids - PIVOTS)[:, None] == column_iota[None, :], own_map[None, :], 0), axis=1
    )
    owner = jnp.where(own_cb, own_target // parent_rows, -1)
    row_iota = jnp.arange(rows, dtype=I32)
    same = (owner[:, None] == owner[None, :]) & (row_iota[None, :] < row_iota[:, None])
    place = jnp.where(own_cb, owner * cap + jnp.sum(same.astype(I32), axis=1), -1)

    high_iota = jnp.arange(parent_width // 128, dtype=I32)
    low_iota = jnp.arange(128, dtype=I32)
    in_high = ((child_map >> 7)[:, :, None] == high_iota).astype(BF16)
    in_low = ((child_map & 127)[:, :, None] == low_iota).astype(BF16)
    counts = jnp.einsum("fah,fal->fhl", in_high, in_low, preferred_element_type=F32)
    within = jnp.einsum(
        "fhl,lm->fhm",
        counts.astype(BF16),
        (low_iota[:, None] < low_iota[None, :]).astype(BF16),
        preferred_element_type=F32,
    )
    totals = jnp.sum(counts, axis=2)
    starts = jnp.einsum(
        "fh,hg->fg",
        totals.astype(BF16),
        (high_iota[:, None] < high_iota[None, :]).astype(BF16),
        preferred_element_type=F32,
    )
    below = starts[:, :, None] + within
    source = jnp.where(counts > 0, below, -1.0).astype(I32).reshape(fronts, parent_width)
    group = starts.astype(I32) >> 7
    own_below = jnp.take(below, my_front, axis=0)
    own_high = ((own_map >> 7)[:, None] == high_iota).astype(F32)
    rank = jnp.sum(
        jnp.where((own_map & 127)[:, None] == low_iota, exact(own_high, own_below), 0.0), axis=1
    ).astype(I32)
    rank = jnp.broadcast_to(rank[:, None], (width, 128))

    factors, outgoing = eliminate(
        own_cb[:, None].astype(I32), place[None, :], rank, inv, inv_rel, front_rows, line, file
    )
    received = lax.all_to_all(
        outgoing.reshape(devices, cap, width), ("front", "helper"), split_axis=0, concat_axis=0, tiled=True
    ).reshape(devices * cap, width)

    own_parent = me * parent_rows + jnp.arange(parent_rows, dtype=I32)
    column = jnp.sum(
        jnp.where(child_map[:, None, :] == own_parent[None, :, None], column_iota + 1, 0), axis=2
    )
    found = column > 0
    stored = jnp.sum(
        jnp.where(
            row_list[:, None, :] == (column + (PIVOTS - 1))[:, :, None],
            jnp.arange(row_list.shape[1], dtype=I32),
            0,
        ),
        axis=2,
    )
    sender = stored // rows
    ahead = jnp.sum(
        (
            found[:, None, :]
            & (sender[:, :, None] == sender[:, None, :])
            & (stored[:, None, :] < stored[:, :, None])
        ).astype(I32),
        axis=2,
    )
    front_iota = jnp.arange(fronts, dtype=I32)
    slot = jnp.where(found, (front_iota[:, None] * helpers + sender) * cap + ahead, -1)
    put = jnp.any(slot[:, :, None] == jnp.arange(devices * cap, dtype=I32), axis=0).astype(BF16)
    assembled = assemble(group, source, put, received, parent)
    return (factors[None], assembled)


def solution(mesh):
    in_specs = (P("front", "helper", None), P(), P(), P(("front", "helper"), None))
    out_specs = (P("front", "helper", None), P(("front", "helper"), None))
    return jax.shard_map(local, mesh=mesh, in_specs=in_specs, out_specs=out_specs, check_vma=False)
```

time: 1470 us -> 257 us (0.17)
  local copies, waits for them, and re-layouts: 995 us -> 27.7 us
  other arithmetic: 402 us -> 7.31 us
  Pallas kernels: 0 us -> 94.3 us
  waiting for transfers between devices: 0.04 us -> 53.1 us
  starting transfers between devices: 11.9 us -> 37.8 us
  blocking collectives: 0 us -> 23.1 us
  between operations: 19.8 us -> 0.95 us
  matrix products: 26.1 us -> 10.6 us
    gather x12 -> x0, local copies, waits for them, and re-layouts: 441 us -> none  [the longest x8 232 us: local(): spread = jnp.take(local_block, jnp.minimum(slot_row, cb_width - 1), axis=1)]
    unnamed x70 -> x28, local copies, waits for them, and re-layouts: 263 us -> 6.69 us
    slice x530 -> x8, local copies, waits for them, and re-layouts: 202 us -> 3.25 us  [the longest x1 0.81 us: spread_panel(): line_up[:middle]]
    div x256 -> x0, other arithmetic: 167 us -> none  [small_inverse(): pivot_row = augmented[column] / augmented[column, column]]
    mul x248 -> x2, other arithmetic: 161 us -> 0.01 us  [the longest x1 0.01 us: local(): relative = (source_x[:, None] * GRID + source_y[None, :]).reshape(helpers)]
    pallas_call x0 -> x4, Pallas kernels: none -> 94.3 us  [the longest x1 36.1 us: eliminate(): pl.pallas_call(eliminate_kernel, out_shape=(jax.ShapeDtypeStruct((rows, c...]
    scatter x257 -> x0, local copies, waits for them, and re-layouts: 57.8 us -> none  [the longest x1 49.8 us: local(): outgoing.at[owner, dest_rank].set(front_rows[:, PIVOTS:], mode='drop')]
    all_to_all x1, waiting for transfers between devices: 0.01 us -> 45.2 us  [local(): lax.all_to_all(outgoing.reshape(devices, cap, width), ('front', 'helper')...]
  transfers between devices with their start and end apart: 2 -> 17, of which waited for: 0 -> 3; matrix products, arithmetic and copies ran while one was open for 32% -> 12% of each run, Pallas kernels for 0% -> 11%
where the time goes in v1:
time: 257 us; the launch traced here: 255 us
  Pallas kernels  94.3 us (37%)
  waiting for transfers between devices  53.1 us (21%)
  starting transfers between devices  37.8 us (15%)
  local copies, waits for them, and re-layouts  27.7 us (11%)
  blocking collectives  23.1 us (9%)
  matrix products  10.6 us (4%)
  other arithmetic  7.31 us (3%)
    all_to_all x1, waiting for transfers between devices, local(): lax.all_to_all(outgoing.reshape(devices, cap, width), ('front', 'helper')...  45.2 us
    pallas_call x1, Pallas kernels, eliminate(): pl.pallas_call(eliminate_kernel, out_shape=(jax.ShapeDtypeStruct((rows, c...  36.1 us
    pallas_call x1, Pallas kernels, invert(): pl.pallas_call(inverse_kernel, out_shape=(jax.ShapeDtypeStruct((PIVOTS, P...  28.3 us
    pallas_call x1, Pallas kernels, assemble(): pl.pallas_call(assemble_kernel, grid_spec=pltpu.PrefetchScalarGridSpec(nu...  25 us
    all_gather x1, blocking collectives, local(): piv = lax.all_gather(pivot, 'helper', axis=0, tiled=True)  23.1 us
    ppermute x16, starting transfers between devices, shift(): return lax.ppermute(value, 'helper', shift_pairs(step))  20.6 us
    all_to_all x1, starting transfers between devices, local(): lax.all_to_all(outgoing.reshape(devices, cap, width), ('front', 'helper')...  17.3 us
    ppermute x16, waiting for transfers between devices, shift(): return lax.ppermute(value, 'helper', shift_pairs(step))  7.97 us
  transfers between devices with their start and end apart: 17, of which 3 were waited for; matrix products, arithmetic and copies ran while one was open for 12% of the time, Pallas kernels for 11%

profile of v1, /device:TPU:1, one launch (start us, length us, event | category | flops | bytes accessed | tf_op | source)
XLA Modules:
  0.0 255.0 jit_solution(560600554579857662)
XLA Ops:
  0.7 1.0 compare_reduce_fusion
  2.3 4.9 %shard_map.68 = (f32[24,256]{1,0:T(8,128)}, f32[24,1920]{1,0:T(8,128)}, f32[24,1920]{1,0:T(8,128)}) custom-call(s32[1,256]{1,0:T(1,128)} %get-tuple-element.52.ids_ref, f32[256,4096]{1,0:T(8,128)} %bitcast.18), custom_call_target="tpu_custom_call" | custom-call | tf_op jit(solution)/shard_map/pallas_call | solution.py:61
  7.1 3.3 %collective-permute-start.1 = (f32[24,1920]{1,0:T(8,128)}, f32[24,1920]{1,0:T(8,128)S(1)}, u32[]{:S(2)}, u32[]{:S(2)}) collective-permute-start(f32[24,1920]{1,0:T(8,128)} %get-tuple-element.12), channel_id=1, source_target_pairs={{0,12},{1,13},{2,14},{3,15},{4,0},{5,1},{6,2},{7,3},{8,4},{9,5},{1... | collective-permute-start | bytes 552968 | tf_op jit(solution)/shard_map/ppermute | solution.py:81
  10.5 2.7 %collective-permute-start.9 = (f32[24,1920]{1,0:T(8,128)}, f32[24,1920]{1,0:T(8,128)S(1)}, u32[]{:S(2)}, u32[]{:S(2)}) collective-permute-start(f32[24,1920]{1,0:T(8,128)} %get-tuple-element.13), channel_id=1, source_target_pairs={{0,3},{1,0},{2,1},{3,2},{4,7},{5,4},{6,5},{7,6},{8,11},{9,8},{10,9... | collective-permute-start | bytes 552968 | tf_op jit(solution)/shard_map/ppermute | solution.py:81
  13.3 1.8 constant_dynamic-update-slice_fusion.4
  15.9 6.5 %fusion.27 = (bf16[8,64]{1,0:T(8,128)(2,1)S(1)}, f32[8,64,128]{2,1,0:T(8,128)S(1)}) fusion(s32[8,3840]{1,0:T(8,128)S(1)} %get-tuple-element.54, s32[8,3840]{1,0:T(8,128)S(1)} %get-tuple-element.53), kind=kOutput, calls=%fused_computation.96 | convolution fusion | flops 509279744 | bytes 508928 | tf_op jit(solution)/shard_map/fah,fal->fhl/dot_general | solution.py:319
  23.4 2.7 %collective-permute-start.3 = (f32[8,1920]{1,0:T(8,128)S(1)}, f32[8,1920]{1,0:T(8,128)S(1)}, u32[]{:S(2)}, u32[]{:S(2)}) collective-permute-start(f32[8,1920]{1,0:T(8,128)S(1)} %slice.56), channel_id=1, source_target_pairs={{0,12},{1,13},{2,14},{3,15},{4,0},{5,1},{6,2},{7,3},{8,4},{9,5},{1... | collective-permute-start | bytes 184328 | tf_op jit(solution)/shard_map/ppermute | solution.py:81
  26.3 2.7 %collective-permute-start.11 = (f32[8,1920]{1,0:T(8,128)S(1)}, f32[8,1920]{1,0:T(8,128)S(1)}, u32[]{:S(2)}, u32[]{:S(2)}) collective-permute-start(f32[8,1920]{1,0:T(8,128)S(1)} %slice.60), channel_id=1, source_target_pairs={{0,3},{1,0},{2,1},{3,2},{4,7},{5,4},{6,5},{7,6},{8,11},{9,8},{10,9... | collective-permute-start | bytes 184328 | tf_op jit(solution)/shard_map/ppermute | solution.py:81
  31.9 2.2 collective-permute-done.10
  35.3 2.6 %collective-permute-start.13 = (f32[96,1920]{1,0:T(8,128)}, f32[96,1920]{1,0:T(8,128)S(1)}, u32[]{:S(2)}, u32[]{:S(2)}) collective-permute-start(f32[96,1920]{1,0:T(8,128)} %constant_dynamic-update-slice_fusion.5.refs_5_), channel_id=1, source_target_pairs={{0,12},{1,13},{2,14},{3,15},{4,0},{5,1},{6,2},{7,3},{8,4},{9,5},{1... | collective-permute-start | bytes 2211848 | tf_op jit(solution)/shard_map/ppermute | solution.py:81
  39.8 1.0 collective-permute-start.4
  40.9 3.0 %fusion.3 = f32[3840]{0:T(1024)S(1)} fusion(s32[3840]{0:T(1024)S(1)} %get-tuple-element.56, s32[3840]{0:T(1024)S(1)} %get-tuple-element.55, f32[8,64,128]{2,1,0:T(8,128)S(1)} %convolution_add_fusion, s32[]{:T(128)S(6)} %select_n.129, pred[]{:T(512)S(6)} %and.116), kind=kOutput, calls=%fused_computation.12 | convolution fusion | flops 379212032 | bytes 80901 | tf_op jit(solution)/shard_map/dot_general | solution.py:24
  44.6 5.7 %collective-permute-done.13.refs_7_ = f32[96,1920]{1,0:T(8,128)S(1)} collective-permute-done((f32[96,1920]{1,0:T(8,128)}, f32[96,1920]{1,0:T(8,128)S(1)}, u32[]{:S(2)}, u32[]{:S(2)}) %collective-permute-start.13) | collective-permute-done | bytes 737312 | tf_op jit(solution)/shard_map/ppermute | solution.py:81
  50.3 0.8 slice.62
  51.1 3.3 %collective-permute-start.15 = (f32[48,1920]{1,0:T(8,128)}, f32[48,1920]{1,0:T(8,128)}, u32[]{:S(2)}, u32[]{:S(2)}) collective-permute-start(f32[48,1920]{1,0:T(8,128)} %slice.62), channel_id=1, source_target_pairs={{0,12},{1,13},{2,14},{3,15},{4,0},{5,1},{6,2},{7,3},{8,4},{9,5},{1... | collective-permute-start | bytes 1105928 | tf_op jit(solution)/shard_map/ppermute | solution.py:81
  54.4 0.8 slice.61
  55.2 0.8 slice.58
  56.0 1.3 collective-permute-start.7
  57.4 0.8 slice.57
  58.3 23.1 %all_gather.3.piv_ref = f32[384,256]{1,0:T(8,128)} all-gather(f32[24,256]{1,0:T(8,128)S(1)} %copy-done.7), channel_id=1, replica_groups=mesh['front'=8,'helper'=16] {'helper'}, dimensions={0}, use_global_device_ids=true | all-gather | bytes 417792 | tf_op jit(solution)/shard_map/all_gather | solution.py:286
  82.7 0.8 copy.8.active_ref
  83.5 28.3 %shard_map.69 = (f32[256,256]{1,0:T(8,128)}, f32[256,384]{1,0:T(8,128)}) custom-call(s32[1,384]{1,0:T(1,128)} %sub.28.slot_abs_ref, s32[1,384]{1,0:T(1,128)} %reshape.192.slot_rel_ref, f32[384,256]{1,0:T(8,128)} %all_gather.3.piv_ref), custom_call_target="tpu_custom_call" | custom-call | tf_op jit(solution)/shard_map/pallas_call | solution.py:134
  112.6 3.0 %broadcast_in_dim.174.rank_ref = s32[3840,128]{1,0:T(8,128)} broadcast(s32[3840]{0:T(1024)S(1)} %convert_element_type.48), dimensions={0} | broadcast | bytes 1981440 | tf_op jit(solution)/shard_map/broadcast_in_dim | solution.py:341
  115.6 36.1 %shard_map.70 = (f32[256,4096]{1,0:T(8,128)}, f32[256,3840]{1,0:T(8,128)}) custom-call(s32[256,1]{1,0:T(8,128)} %copy.8.active_ref, s32[1,256]{1,0:T(1,128)} %bitcast.21, s32[3840,128]{1,0:T(8,128)} %broadcast_in_dim.174.rank_ref, f32[256,256]{1,0:T(8,128)} %get-tuple-element.10.inv_ref, f32[256,384]{1,0:T(8,128)} %get-tuple-element.11.inv_rel_ref, ...), custom_call_target="tpu_custom_call" | custom-call | tf_op jit(solution)/shard_map/pallas_call | solution.py:205
  151.8 5.5 %reshape.194 = f32[128,2,3840]{2,1,0:T(2,128)} reshape(f32[256,3840]{1,0:T(8,128)} %get-tuple-element.15) | data formatting | bytes 7864320 | tf_op jit(solution)/shard_map/reshape | solution.py:347
  157.3 17.3 %all-to-all-start = ((f32[128,2,3840]{2,1,0:T(2,128)}), f32[128,2,3840]{2,1,0:T(2,128)}, u32[]{:S(2)}, u32[]{:S(2)}) async-start(f32[128,2,3840]{2,1,0:T(2,128)} %reshape.194), calls=%async_computation | async-start | bytes 7864320 | tf_op jit(solution)/shard_map/all_to_all | solution.py:346
  174.7 1.0 select_reduce_fusion.1
  175.7 1.3 select_reduce_fusion
  178.2 0.9 copy.11
  179.1 45.2 %all-to-all-done = f32[128,2,3840]{2,1,0:T(2,128)} async-done(((f32[128,2,3840]{2,1,0:T(2,128)}), f32[128,2,3840]{2,1,0:T(2,128)}, u32[]{:S(2)}, u32[]{:S(2)}) %all-to-all-start) | async-done | bytes 3932192 | tf_op jit(solution)/shard_map/all_to_all | solution.py:346
  224.2 5.7 %reshape.195.received_ref = f32[256,3840]{1,0:T(8,128)} reshape(f32[128,2,3840]{2,1,0:T(2,128)} %all-to-all-done) | data formatting | bytes 7864320 | tf_op jit(solution)/shard_map/reshape | solution.py:348
  229.9 25.0 %shard_map.71 = f32[64,8192]{1,0:T(8,128)} custom-call(s32[8,64]{1,0:T(8,128)} %get-tuple-element.61.group_ref, s32[8,8192]{1,0:T(8,128)} %bitcast.20, bf16[64,256]{1,0:T(8,128)(2,1)} %convert_element_type.53.put_ref, f32[256,3840]{1,0:T(8,128)} %reshape.195.received_ref, f32[64,8192]{1,0:T(8,128)} %parent_ref.1), custom_call_target="tpu_custom_call" | custom-call | tf_op jit(solution)/shard_map/pallas_call | solution.py:251
  (91 shorter events, 12.7 us)
Async XLA Ops:
  0.6 14.5 %copy-start.9 = (s32[4]{0:T(128)S(1)}, s32[4]{0:T(128)}, u32[]{:S(2)}) copy-start(s32[4]{0:T(128)} %constant.152.clone) | copy-start | bytes 52
  0.6 12.6 %copy-start.4 = (s32[8,3840]{1,0:T(8,128)S(1)}, s32[8,3840]{1,0:T(8,128)}, u32[]{:S(2)}) copy-start(s32[8,3840]{1,0:T(8,128)} %param.7) | copy-start | bytes 368644
  7.1 16.3 %collective-permute-start.1 = (f32[24,1920]{1,0:T(8,128)}, f32[24,1920]{1,0:T(8,128)S(1)}, u32[]{:S(2)}, u32[]{:S(2)}) collective-permute-start(f32[24,1920]{1,0:T(8,128)} %get-tuple-element.12), channel_id=1, source_target_pairs={{0,12},{1,13},{2,14},{3,15},{4,0},{5,1},{6,2},{7,3},{8,4},{9,5},{1... | collective-permute-start | bytes 552968 | tf_op jit(solution)/shard_map/ppermute | solution.py:81
  10.5 15.7 %collective-permute-start = (f32[24,1920]{1,0:T(8,128)}, f32[24,1920]{1,0:T(8,128)S(1)}, u32[]{:S(2)}, u32[]{:S(2)}) collective-permute-start(f32[24,1920]{1,0:T(8,128)} %get-tuple-element.12), channel_id=1, source_target_pairs={{0,4},{1,5},{2,6},{3,7},{4,8},{5,9},{6,10},{7,11},{8,12},{9,13},{1... | collective-permute-start | bytes 552968 | tf_op jit(solution)/shard_map/ppermute | solution.py:81
  10.5 15.8 %collective-permute-start.9 = (f32[24,1920]{1,0:T(8,128)}, f32[24,1920]{1,0:T(8,128)S(1)}, u32[]{:S(2)}, u32[]{:S(2)}) collective-permute-start(f32[24,1920]{1,0:T(8,128)} %get-tuple-element.13), channel_id=1, source_target_pairs={{0,3},{1,0},{2,1},{3,2},{4,7},{5,4},{6,5},{7,6},{8,11},{9,8},{10,9... | collective-permute-start | bytes 552968 | tf_op jit(solution)/shard_map/ppermute | solution.py:81
  13.2 15.8 %collective-permute-start.8 = (f32[24,1920]{1,0:T(8,128)}, f32[24,1920]{1,0:T(8,128)S(1)}, u32[]{:S(2)}, u32[]{:S(2)}) collective-permute-start(f32[24,1920]{1,0:T(8,128)} %get-tuple-element.13), channel_id=1, source_target_pairs={{0,1},{1,2},{2,3},{3,0},{4,5},{5,6},{6,7},{7,4},{8,9},{9,10},{10,1... | collective-permute-start | bytes 552968 | tf_op jit(solution)/shard_map/ppermute | solution.py:81
  15.9 24.9 %copy-start.8 = (s32[1,256]{1,0:T(1,128)S(1)}, s32[1,256]{1,0:T(1,128)}, u32[]{:S(2)}) copy-start(s32[1,256]{1,0:T(1,128)} %get-tuple-element.52.ids_ref) | copy-start | bytes 3076
  23.4 15.2 %collective-permute-start.3 = (f32[8,1920]{1,0:T(8,128)S(1)}, f32[8,1920]{1,0:T(8,128)S(1)}, u32[]{:S(2)}, u32[]{:S(2)}) collective-permute-start(f32[8,1920]{1,0:T(8,128)S(1)} %slice.56), channel_id=1, source_target_pairs={{0,12},{1,13},{2,14},{3,15},{4,0},{5,1},{6,2},{7,3},{8,4},{9,5},{1... | collective-permute-start | bytes 184328 | tf_op jit(solution)/shard_map/ppermute | solution.py:81
  26.2 11.8 %collective-permute-start.2 = (f32[16,1920]{1,0:T(8,128)S(1)}, f32[16,1920]{1,0:T(8,128)S(1)}, u32[]{:S(2)}, u32[]{:S(2)}) collective-permute-start(f32[16,1920]{1,0:T(8,128)S(1)} %slice.55), channel_id=1, source_target_pairs={{0,4},{1,5},{2,6},{3,7},{4,8},{5,9},{6,10},{7,11},{8,12},{9,13},{1... | collective-permute-start | bytes 368648 | tf_op jit(solution)/shard_map/ppermute | solution.py:81
  26.3 32.0 %copy-start.7 = (f32[24,256]{1,0:T(8,128)S(1)}, f32[24,256]{1,0:T(8,128)}, u32[]{:S(2)}) copy-start(f32[24,256]{1,0:T(8,128)} %get-tuple-element.9) | copy-start | bytes 73732
  26.3 8.4 %collective-permute-start.11 = (f32[8,1920]{1,0:T(8,128)S(1)}, f32[8,1920]{1,0:T(8,128)S(1)}, u32[]{:S(2)}, u32[]{:S(2)}) collective-permute-start(f32[8,1920]{1,0:T(8,128)S(1)} %slice.60), channel_id=1, source_target_pairs={{0,3},{1,0},{2,1},{3,2},{4,7},{5,4},{6,5},{7,6},{8,11},{9,8},{10,9... | collective-permute-start | bytes 184328 | tf_op jit(solution)/shard_map/ppermute | solution.py:81
  29.0 5.0 %collective-permute-start.10 = (f32[16,1920]{1,0:T(8,128)S(1)}, f32[16,1920]{1,0:T(8,128)S(1)}, u32[]{:S(2)}, u32[]{:S(2)}) collective-permute-start(f32[16,1920]{1,0:T(8,128)S(1)} %slice.59), channel_id=1, source_target_pairs={{0,1},{1,2},{2,3},{3,0},{4,5},{5,6},{6,7},{7,4},{8,9},{9,10},{10,1... | collective-permute-start | bytes 368648 | tf_op jit(solution)/shard_map/ppermute | solution.py:81
  35.3 15.0 %collective-permute-start.13 = (f32[96,1920]{1,0:T(8,128)}, f32[96,1920]{1,0:T(8,128)S(1)}, u32[]{:S(2)}, u32[]{:S(2)}) collective-permute-start(f32[96,1920]{1,0:T(8,128)} %constant_dynamic-update-slice_fusion.5.refs_5_), channel_id=1, source_target_pairs={{0,12},{1,13},{2,14},{3,15},{4,0},{5,1},{6,2},{7,3},{8,4},{9,5},{1... | collective-permute-start | bytes 2211848 | tf_op jit(solution)/shard_map/ppermute | solution.py:81
  38.0 16.4 %collective-permute-start.12 = (f32[96,1920]{1,0:T(8,128)}, f32[96,1920]{1,0:T(8,128)S(1)}, u32[]{:S(2)}, u32[]{:S(2)}) collective-permute-start(f32[96,1920]{1,0:T(8,128)} %constant_dynamic-update-slice_fusion.5.refs_5_), channel_id=1, source_target_pairs={{0,4},{1,5},{2,6},{3,7},{4,8},{5,9},{6,10},{7,11},{8,12},{9,13},{1... | collective-permute-start | bytes 2211848 | tf_op jit(solution)/shard_map/ppermute | solution.py:81
  39.3 15.9 %collective-permute-start.5 = (f32[96,1920]{1,0:T(8,128)}, f32[96,1920]{1,0:T(8,128)S(1)}, u32[]{:S(2)}, u32[]{:S(2)}) collective-permute-start(f32[96,1920]{1,0:T(8,128)} %constant_dynamic-update-slice_fusion.refs_0_), channel_id=1, source_target_pairs={{0,3},{1,0},{2,1},{3,2},{4,7},{5,4},{6,5},{7,6},{8,11},{9,8},{10,9... | collective-permute-start | bytes 2211848 | tf_op jit(solution)/shard_map/ppermute | solution.py:81
  39.8 17.6 %collective-permute-start.4 = (f32[96,1920]{1,0:T(8,128)}, f32[96,1920]{1,0:T(8,128)S(1)}, u32[]{:S(2)}, u32[]{:S(2)}) collective-permute-start(f32[96,1920]{1,0:T(8,128)} %constant_dynamic-update-slice_fusion.refs_0_), channel_id=1, source_target_pairs={{0,1},{1,2},{2,3},{3,0},{4,5},{5,6},{6,7},{7,4},{8,9},{9,10},{10,1... | collective-permute-start | bytes 2211848 | tf_op jit(solution)/shard_map/ppermute | solution.py:81
  50.3 65.3 %copy-start = (f32[96,1920]{1,0:T(8,128)}, f32[96,1920]{1,0:T(8,128)S(1)}, u32[]{:S(2)}) copy-start(f32[96,1920]{1,0:T(8,128)S(1)} %collective-permute-done.13.refs_7_) | copy-start | bytes 2211844
  51.1 61.5 %collective-permute-start.15 = (f32[48,1920]{1,0:T(8,128)}, f32[48,1920]{1,0:T(8,128)}, u32[]{:S(2)}, u32[]{:S(2)}) collective-permute-start(f32[48,1920]{1,0:T(8,128)} %slice.62), channel_id=1, source_target_pairs={{0,12},{1,13},{2,14},{3,15},{4,0},{5,1},{6,2},{7,3},{8,4},{9,5},{1... | collective-permute-start | bytes 1105928 | tf_op jit(solution)/shard_map/ppermute | solution.py:81
  54.4 61.2 %copy-start.1 = (f32[96,1920]{1,0:T(8,128)}, f32[96,1920]{1,0:T(8,128)S(1)}, u32[]{:S(2)}) copy-start(f32[96,1920]{1,0:T(8,128)S(1)} %collective-permute-done.12.refs_6_) | copy-start | bytes 2211844
  55.2 57.3 %collective-permute-start.14 = (f32[48,1920]{1,0:T(8,128)}, f32[48,1920]{1,0:T(8,128)}, u32[]{:S(2)}, u32[]{:S(2)}) collective-permute-start(f32[48,1920]{1,0:T(8,128)} %slice.61), channel_id=1, source_target_pairs={{0,4},{1,5},{2,6},{3,7},{4,8},{5,9},{6,10},{7,11},{8,12},{9,13},{1... | collective-permute-start | bytes 1105928 | tf_op jit(solution)/shard_map/ppermute | solution.py:81
  55.2 60.4 %copy-start.2 = (f32[96,1920]{1,0:T(8,128)}, f32[96,1920]{1,0:T(8,128)S(1)}, u32[]{:S(2)}) copy-start(f32[96,1920]{1,0:T(8,128)S(1)} %collective-permute-done.5.refs_2_) | copy-start | bytes 2211844
  56.0 56.5 %collective-permute-start.7 = (f32[48,1920]{1,0:T(8,128)}, f32[48,1920]{1,0:T(8,128)}, u32[]{:S(2)}, u32[]{:S(2)}) collective-permute-start(f32[48,1920]{1,0:T(8,128)} %slice.58), channel_id=1, source_target_pairs={{0,3},{1,0},{2,1},{3,2},{4,7},{5,4},{6,5},{7,6},{8,11},{9,8},{10,9... | collective-permute-start | bytes 1105928 | tf_op jit(solution)/shard_map/ppermute | solution.py:81
  57.4 58.3 %copy-start.3 = (f32[96,1920]{1,0:T(8,128)}, f32[96,1920]{1,0:T(8,128)S(1)}, u32[]{:S(2)}) copy-start(f32[96,1920]{1,0:T(8,128)S(1)} %collective-permute-done.4.refs_1_) | copy-start | bytes 2211844
  58.2 54.4 %collective-permute-start.6 = (f32[48,1920]{1,0:T(8,128)}, f32[48,1920]{1,0:T(8,128)}, u32[]{:S(2)}, u32[]{:S(2)}) collective-permute-start(f32[48,1920]{1,0:T(8,128)} %slice.57), channel_id=1, source_target_pairs={{0,1},{1,2},{2,3},{3,0},{4,5},{5,6},{6,7},{7,4},{8,9},{9,10},{10,1... | collective-permute-start | bytes 1105928 | tf_op jit(solution)/shard_map/ppermute | solution.py:81
  157.3 17.3 %copy-start.5 = (s32[8,3840]{1,0:T(8,128)S(1)}, s32[8,3840]{1,0:T(8,128)}, u32[]{:S(2)}) copy-start(s32[8,3840]{1,0:T(8,128)} %param.7) | copy-start | bytes 368644
  157.3 18.3 %copy-start.6 = (s32[8,4096]{1,0:T(8,128)S(1)}, s32[8,4096]{1,0:T(8,128)}, u32[]{:S(2)}) copy-start(s32[8,4096]{1,0:T(8,128)} %param.6) | copy-start | bytes 393220
  157.3 66.9 %all-to-all-start = ((f32[128,2,3840]{2,1,0:T(2,128)}), f32[128,2,3840]{2,1,0:T(2,128)}, u32[]{:S(2)}, u32[]{:S(2)}) async-start(f32[128,2,3840]{2,1,0:T(2,128)} %reshape.194), calls=%async_computation | async-start | bytes 7864320 | tf_op jit(solution)/shard_map/all_to_all | solution.py:346

commit v2 on v1

v2 whole, which is shorter than its diff:
```python
import jax
import jax.numpy as jnp
from jax import lax
from jax.experimental import pallas as pl
from jax.experimental.pallas import tpu as pltpu
from jax.sharding import PartitionSpec as P

PIVOTS = 256
CAP = 24
BASE = 32
F32 = jnp.float32
BF16 = jnp.bfloat16
I32 = jnp.int32
GRID = 4
X_UP, X_DOWN, X_FAR = (1, 0), (3, 0), (2, 0)
Y_UP, Y_DOWN, Y_FAR = (0, 1), (0, 3), (0, 2)
BIG = pltpu.CompilerParams(vmem_limit_bytes=58 << 20)


def iota(shape, axis):
    return lax.broadcasted_iota(I32, shape, axis)


def exact(left, right):
    return jnp.dot(left, right, precision=lax.Precision.HIGHEST, preferred_element_type=F32)


def halves(value):
    high = value.astype(BF16)
    return high, (value - high.astype(F32)).astype(BF16)


def dot16(left, right):
    return jnp.dot(left, right, preferred_element_type=F32)


def dot3(left, right):
    left_high, left_low = halves(left)
    right_high, right_low = halves(right)
    return dot16(left_high, right_high) + (dot16(left_high, right_low) + dot16(left_low, right_high))


def select_kernel(ids_ref, front_ref, pivot_ref, first_ref, second_ref):
    rows = front_ref.shape[0]
    ids = ids_ref[...]
    inside = jnp.broadcast_to((ids < PIVOTS).astype(F32), (8, rows)).astype(BF16)
    before = (iota((rows, rows), 0) < iota((rows, rows), 1)).astype(F32).astype(BF16)
    rank = dot16(inside, before)[:1].astype(I32)
    rank = jnp.where(ids < PIVOTS, rank, -1)
    chosen = (jnp.broadcast_to(rank, (CAP, rows)) == iota((CAP, rows), 0)).astype(F32).astype(BF16)

    def pick(start, into):
        step = 512
        for at in range(0, into.shape[1], step):
            stop = min(at + step, into.shape[1])
            value = front_ref[:, start + at : start + stop]
            high = value.astype(BF16)
            middle, low = halves(value - high.astype(F32))
            into[:, at:stop] = dot16(chosen, high) + (dot16(chosen, middle) + dot16(chosen, low))

    pick(0, pivot_ref)
    pick(PIVOTS, first_ref)
    pick(PIVOTS + first_ref.shape[1], second_ref)


def select_panel(own_ids, front_rows):
    half = (front_rows.shape[1] - PIVOTS) // 2
    return pl.pallas_call(
        select_kernel,
        out_shape=(
            jax.ShapeDtypeStruct((CAP, PIVOTS), F32),
            jax.ShapeDtypeStruct((CAP, half), F32),
            jax.ShapeDtypeStruct((CAP, half), F32),
        ),
        compiler_params=BIG,
    )(own_ids[None, :], front_rows)


def shift_pairs(step):
    return [
        (x * GRID + y, (x + step[0]) % GRID * GRID + (y + step[1]) % GRID)
        for x in range(GRID)
        for y in range(GRID)
    ]


def shift(value, step):
    return lax.ppermute(value, "helper", shift_pairs(step))


def pack_kernel(*refs):
    for index in range(8):
        into = slice(index % 2 * CAP, (index % 2 + 1) * CAP)
        refs[8 + index // 2][into, :] = refs[index][...]


def pack(firsts, seconds):
    half = seconds[0].shape[1]
    return pl.pallas_call(
        pack_kernel,
        out_shape=(jax.ShapeDtypeStruct((2 * CAP, half), F32),) * 4,
        compiler_params=BIG,
    )(*firsts, *seconds)


def rank_kernel(map_ref, rank_ref):
    width = map_ref.shape[1]
    high = (iota((64, width), 0) == (map_ref[...] >> 7)).astype(F32).astype(BF16)
    in_low = iota((128, width), 0) == (map_ref[...] & 127)
    low = in_low.astype(F32).astype(BF16)
    counts = lax.dot_general(high, low, (((1,), (1,)), ((), ())), preferred_element_type=F32)
    before = (iota((128, 128), 0) < iota((128, 128), 1)).astype(F32).astype(BF16)
    within = dot16(counts.astype(BF16), before)
    earlier = (iota((64, 64), 1) < iota((64, 64), 0)).astype(F32).astype(BF16)
    starts = jnp.sum(dot16(earlier, counts.astype(BF16)), axis=1, keepdims=True)
    below = (starts + within).astype(I32)
    coarse = (below >> 6).astype(F32).astype(BF16)
    fine = (below & 63).astype(F32).astype(BF16)
    contract = (((0,), (0,)), ((), ()))
    table = 64.0 * lax.dot_general(coarse, high, contract, preferred_element_type=F32)
    table = table + lax.dot_general(fine, high, contract, preferred_element_type=F32)
    row = jnp.sum(jnp.where(in_low, table, 0.0), axis=0, keepdims=True)
    for start in range(0, width, 128):
        block = jnp.broadcast_to(row[:, start : start + 128], (128, 128))
        rank_ref[start : start + 128, :] = block.T.astype(I32)


def column_ranks(own_map):
    width = own_map.shape[0]
    return pl.pallas_call(
        rank_kernel, out_shape=jax.ShapeDtypeStruct((width, 128), I32), compiler_params=BIG
    )(own_map[None, :])


def inverse_kernel(slot_abs_ref, slot_rel_ref, piv_ref, inv_ref, inv_rel_ref):
    slots = piv_ref.shape[0]
    natural = (iota((PIVOTS, slots), 0) == slot_abs_ref[...]).astype(F32)
    inv_ref[...] = exact(natural, piv_ref[...])
    lanes = iota((1, PIVOTS), 1)
    for block in range(PIVOTS // BASE):
        base = block * BASE
        rows = inv_ref[base : base + BASE, :]
        sub = iota((BASE, 1), 0)
        for step in range(BASE):
            at = base + step
            here = lanes == at
            pivot_row = rows[step : step + 1, :]
            if step == 0:
                column = jnp.broadcast_to(rows[:, at : at + 1], (BASE, 128))
                following = jnp.broadcast_to(rows[:, at + 1 : at + 2], (BASE, 128))
            recip = 1.0 / column[step : step + 1, :]
            if step + 2 < BASE:
                ahead = jnp.broadcast_to(rows[:, at + 2 : at + 3], (BASE, 128))
            scaled = jnp.where(here, 1.0, pivot_row) * jnp.concatenate([recip, recip], axis=1)
            both = jnp.concatenate([column, column], axis=1)
            rows = jnp.where(sub == step, scaled, jnp.where(here, 0.0, rows) - both * scaled)

            def turn(value):
                turned = value[step : step + 1, :] * recip
                return jnp.where(sub == step, turned, value - column * turned)

            if step + 1 < BASE:
                turned_next = turn(following)
                if step + 2 < BASE:
                    following = turn(ahead)
                column = turned_next
        in_block = (lanes >= base) & (lanes < base + BASE)
        full = inv_ref[...]
        left = jnp.where(in_block, full, 0.0)
        kept = jnp.where(in_block, 0.0, full)
        parts = []
        if base:
            parts.append(jnp.zeros((base, PIVOTS), F32))
        parts.append(rows)
        if base + BASE < PIVOTS:
            parts.append(jnp.zeros((PIVOTS - base - BASE, PIVOTS), F32))
        inv_ref[...] = kept - exact(left, jnp.concatenate(parts, axis=0))
        inv_ref[base : base + BASE, :] = rows
    relative = (iota((PIVOTS, slots), 0) == slot_rel_ref[...]).astype(F32)
    inv_rel_ref[...] = exact(inv_ref[...], relative)


def invert(slot_abs, slot_rel, piv):
    slots = piv.shape[0]
    return pl.pallas_call(
        inverse_kernel,
        out_shape=(
            jax.ShapeDtypeStruct((PIVOTS, PIVOTS), F32),
            jax.ShapeDtypeStruct((PIVOTS, slots), F32),
        ),
        compiler_params=BIG,
    )(slot_abs, slot_rel, piv)


OFFSETS = (0, 3, 1, 2)


def eliminate_kernel(
    active_ref, place_ref, inv_ref, inv_rel_ref, rank_hbm, front_hbm, *refs
):
    pieces, refs = refs[:16], refs[16:]
    factors_hbm, send_hbm = refs[:2]
    matrix, upper, ranks, sorted_in, moves, send = refs[2:8]
    front_sem, upper_sem, rank_sem, factors_sem, send_sem = refs[8:]
    rows, columns = matrix.shape
    width = columns - PIVOTS
    half = width // 2
    tile = 256
    tiles = width // tile

    loads = [pltpu.make_async_copy(front_hbm.at[:, :PIVOTS], matrix.at[:, :PIVOTS], front_sem.at[0])]
    for part in range(2):
        at = PIVOTS + part * half
        loads.append(
            pltpu.make_async_copy(front_hbm.at[:, at : at + half], matrix.at[:, at : at + half], front_sem.at[part + 1])
        )
    rank_load = pltpu.make_async_copy(rank_hbm, ranks, rank_sem)
    upper_loads = []
    for part in range(2):
        into = slice(part * half, (part + 1) * half)
        for piece in range(4):
            for block in range(4):
                source, at = pieces[part * 8 + piece * 2 + block // 2], block % 2 * CAP
                slot = ((block * 4 + piece) if part == 0 else (piece * 4 + block)) * CAP
                upper_loads.append(
                    pltpu.make_async_copy(
                        source.at[at : at + CAP, :], upper.at[slot : slot + CAP, into], upper_sem.at[part * 16 + piece * 4 + block]
                    )
                )
    loads[0].start()
    loads[1].start()
    for load in upper_loads[:16]:
        load.start()
    loads[2].start()
    for load in upper_loads[16:]:
        load.start()
    rank_load.start()

    loads[0].wait()
    active = active_ref[...] > 0
    current = matrix[:, :PIVOTS]
    lower = jnp.where(active, dot3(current, inv_rel_ref[...]), 0.0)
    lower_high, lower_low = halves(lower)
    lower_both = jnp.concatenate([lower_high, lower_low], axis=0)
    matrix[:, :PIVOTS] = jnp.where(active, dot3(current, inv_ref[...]), current)
    stores = [pltpu.make_async_copy(matrix.at[:, :PIVOTS], factors_hbm.at[:, :PIVOTS], factors_sem.at[0])]
    stores[0].start()
    place = (iota((rows, rows), 0) == place_ref[...]).astype(F32).astype(BF16)

    def update(at, size):
        high, low = halves(upper[:, pl.ds(at, size)])
        change = dot16(lower_both, high)
        change = change[:rows] + (change[rows:] + dot16(lower_high, low))
        out = matrix[:, pl.ds(at + PIVOTS, size)] - change
        matrix[:, pl.ds(at + PIVOTS, size)] = out
        high, low = halves(out)
        placed = dot16(place, jnp.concatenate([high, low], axis=1)).astype(BF16)
        sorted_in[:rows, pl.ds(at, size)] = placed[:, :size]
        sorted_in[rows:, pl.ds(at, size)] = placed[:, size:]

    def generate(slot, index):
        lane = iota((1, 128), 1) + index * tile
        for part in range(2):
            moves[slot, :, part * 128 : (part + 1) * 128] = (
                (ranks[...] == lane + part * 128).astype(F32).astype(BF16)
            )

    for part in range(2):
        loads[part + 1].wait()
        for load in upper_loads[part * 16 : part * 16 + 16]:
            load.wait()

        def updates(index, carry):
            update(pl.multiple_of(part * half + index * 384, 128), 384)
            return carry

        lax.fori_loop(0, half // 384, updates, 0)
        at = PIVOTS + part * half
        stores.append(
            pltpu.make_async_copy(matrix.at[:, at : at + half], factors_hbm.at[:, at : at + half], factors_sem.at[part + 1])
        )
        stores[-1].start()

    rank_load.wait()
    generate(0, 0)

    def permute(slot, index):
        at = pl.multiple_of(index * tile, tile)
        out = dot16(sorted_in[...], moves[slot])
        send[:, :, pl.ds(at, tile)] = (out[:rows] + out[rows:]).reshape(rows // 2, 2, tile)
        pltpu.make_async_copy(
            send.at[:, :, pl.ds(at, tile)], send_hbm.at[:, :, pl.ds(at, tile)], send_sem.at[index]
        ).start()

    def pair(index, carry):
        generate(1, 2 * index + 1)
        permute(0, 2 * index)
        generate(0, 2 * index + 2)
        permute(1, 2 * index + 1)
        return carry

    lax.fori_loop(0, tiles // 2, pair, 0)
    permute(0, tiles - 1)
    for store in stores:
        store.wait()
    for index in range(tiles):
        at = index * tile
        pltpu.make_async_copy(
            send.at[:, :, at : at + tile], send_hbm.at[:, :, at : at + tile], send_sem.at[index]
        ).wait()


def eliminate(active, place, rank, inv, inv_rel, front_rows, line, file):
    rows, columns = front_rows.shape
    width = columns - PIVOTS
    vmem = pl.BlockSpec(memory_space=pltpu.VMEM)
    hbm = pl.BlockSpec(memory_space=pl.ANY)
    return pl.pallas_call(
        eliminate_kernel,
        in_specs=[vmem] * 4 + [hbm] * 18,
        out_specs=(hbm, hbm),
        out_shape=(
            jax.ShapeDtypeStruct((rows, columns), F32),
            jax.ShapeDtypeStruct((rows // 2, 2, width), F32),
        ),
        scratch_shapes=[
            pltpu.VMEM((rows, columns), F32),
            pltpu.VMEM((16 * CAP, width), F32),
            pltpu.VMEM(rank.shape, I32),
            pltpu.VMEM((2 * rows, width), BF16),
            pltpu.VMEM((2, width, 256), BF16),
            pltpu.VMEM((rows // 2, 2, width), F32),
            pltpu.SemaphoreType.DMA((3,)),
            pltpu.SemaphoreType.DMA((32,)),
            pltpu.SemaphoreType.DMA,
            pltpu.SemaphoreType.DMA((3,)),
            pltpu.SemaphoreType.DMA((width // 256,)),
        ],
        compiler_params=BIG,
    )(active, place, inv, inv_rel, rank, front_rows, *line, *file)


def assemble_kernel(group_ref, source_ref, put_ref, received_ref, parent_ref, out_ref):
    fronts = source_ref.shape[0]
    senders = received_ref.shape[0] // fronts
    per_front = senders * received_ref.shape[1]
    last = received_ref.shape[2] // 128 - 1
    first = pl.program_id(0) * (out_ref.shape[1] // 128)
    put = put_ref[...]
    for tile in range(out_ref.shape[1] // 256):
        columns = []
        for part in (2 * tile, 2 * tile + 1):
            pieces = []
            for front in range(fronts):
                group = jnp.minimum(group_ref[front, first + part], last)
                following = jnp.minimum(group + 1, last)
                source = source_ref[front : front + 1, part * 128 : (part + 1) * 128]
                lane = jnp.broadcast_to(source & 127, (per_front, 128))
                which = source >> 7
                span = slice(front * senders, (front + 1) * senders)
                near = received_ref[span, :, pl.ds(pl.multiple_of(group * 128, 128), 128)].reshape(per_front, 128)
                far = received_ref[span, :, pl.ds(pl.multiple_of(following * 128, 128), 128)].reshape(per_front, 128)
                near = jnp.take_along_axis(near, lane, axis=1)
                far = jnp.take_along_axis(far, lane, axis=1)
                pieces.append(jnp.where(which == group, near, jnp.where(which == following, far, 0.0)))
            columns.append(jnp.concatenate(pieces, axis=0))
        high, low = halves(jnp.concatenate(columns, axis=1))
        at = slice(tile * 256, (tile + 1) * 256)
        out_ref[:, at] = parent_ref[:, at] + (dot16(put, high) + dot16(put, low))


def assemble(group, source, put, received, parent):
    rows, width = parent.shape
    fronts = source.shape[0]
    tile = 2048
    return pl.pallas_call(
        assemble_kernel,
        grid_spec=pltpu.PrefetchScalarGridSpec(
            num_scalar_prefetch=1,
            grid=(width // tile,),
            in_specs=[
                pl.BlockSpec((fronts, tile), lambda i, g: (0, i)),
                pl.BlockSpec(put.shape, lambda i, g: (0, 0)),
                pl.BlockSpec(received.shape, lambda i, g: (0, 0, 0)),
                pl.BlockSpec((rows, tile), lambda i, g: (0, i)),
            ],
            out_specs=pl.BlockSpec((rows, tile), lambda i, g: (0, i)),
        ),
        out_shape=jax.ShapeDtypeStruct((rows, width), F32),
        compiler_params=BIG,
    )(group, source, put, received, parent)


def columns_below(child_map, parent_width):
    high_iota = jnp.arange(parent_width // 128, dtype=I32)
    low_iota = jnp.arange(128, dtype=I32)
    in_high = ((child_map >> 7)[:, :, None] == high_iota).astype(BF16)
    in_low = ((child_map & 127)[:, :, None] == low_iota).astype(BF16)
    counts = jnp.einsum("fah,fal->fhl", in_high, in_low, preferred_element_type=F32)
    within = jnp.einsum(
        "fhl,lm->fhm",
        counts.astype(BF16),
        (low_iota[:, None] < low_iota[None, :]).astype(BF16),
        preferred_element_type=F32,
    )
    starts = jnp.einsum(
        "fh,hg->fg",
        jnp.sum(counts, axis=2).astype(BF16),
        (high_iota[:, None] < high_iota[None, :]).astype(BF16),
        preferred_element_type=F32,
    )
    return starts[:, :, None] + within, counts


def local(front, row_list, child_map, parent):
    front_rows = front[0]
    rows = front_rows.shape[0]
    width = front_rows.shape[1] - PIVOTS
    helpers = lax.axis_size("helper")
    fronts = lax.axis_size("front")
    devices = helpers * fronts
    cap = (rows + devices - 1) // devices
    parent_rows, parent_width = parent.shape
    my_front = lax.axis_index("front")
    my_helper = lax.axis_index("helper")
    me = my_front * helpers + my_helper
    order = jnp.take(row_list, my_front, axis=0)
    by_helper = order.reshape(helpers, rows)
    own_ids = lax.dynamic_slice_in_dim(order, my_helper * rows, rows)

    pivot, first, second = select_panel(own_ids, front_rows)
    own_map = jnp.take(child_map, my_front, axis=0)
    piv = lax.all_to_all(
        jnp.broadcast_to(pivot[None], (helpers, CAP, PIVOTS)), "helper", split_axis=0, concat_axis=0, tiled=True
    ).reshape(helpers * CAP, PIVOTS)
    firsts = (first, shift(first, X_UP), shift(first, X_DOWN), shift(first, X_FAR))
    seconds = (second, shift(second, Y_UP), shift(second, Y_DOWN), shift(second, Y_FAR))

    inside = by_helper < PIVOTS
    earlier = (jnp.arange(rows)[:, None] < jnp.arange(rows)[None, :]).astype(BF16)
    slot_rank = dot16(inside.astype(BF16), earlier).astype(I32)
    slot_iota = jnp.arange(CAP, dtype=I32)
    hit = (slot_rank[:, None, :] == slot_iota[None, :, None]) & inside[:, None, :]
    slot_row = jnp.sum(jnp.where(hit, by_helper[:, None, :] + 1, 0), axis=2) - 1
    grid_iota = jnp.array(OFFSETS, I32)
    source_x = (my_helper // GRID + grid_iota) % GRID
    source_y = (my_helper % GRID + grid_iota) % GRID
    relative = (source_x[:, None] * GRID + source_y[None, :]).reshape(helpers)
    slot_rel = jnp.sum(
        jnp.where((relative[:, None] == jnp.arange(helpers)[None, :])[:, :, None], slot_row[None], 0), axis=1
    )
    rank = column_ranks(own_map)
    slot_row, slot_rel = slot_row.reshape(1, -1), slot_rel.reshape(1, -1)
    firsts, seconds, rank, slot_row, slot_rel = lax.optimization_barrier((firsts, seconds, rank, slot_row, slot_rel))

    line_a, line_b, file_a, file_b = pack(firsts, seconds)
    line_up, line_down = shift(line_a, Y_UP), shift(line_b, Y_DOWN)
    file_up, file_down = shift(file_a, X_UP), shift(file_b, X_DOWN)
    line_rest = shift(line_b, Y_UP), shift(line_a, Y_DOWN)
    file_rest = shift(file_b, X_UP), shift(file_a, X_DOWN)
    inv, inv_rel = invert(slot_row, slot_rel, piv)
    line_up, line_down, file_up, file_down, inv, inv_rel = lax.optimization_barrier(
        (line_up, line_down, file_up, file_down, inv, inv_rel)
    )
    line = (line_a, line_b, line_up, line_rest[0], line_rest[1], line_down, shift(line_up, Y_UP), shift(line_down, Y_DOWN))
    file = (file_a, file_b, file_up, file_rest[0], file_rest[1], file_down, shift(file_up, X_UP), shift(file_down, X_DOWN))

    own_cb = own_ids >= PIVOTS
    column_iota = jnp.arange(width, dtype=I32)
    own_target = jnp.sum(
        jnp.where((own_ids - PIVOTS)[:, None] == column_iota[None, :], own_map[None, :], 0), axis=1
    )
    owner = jnp.where(own_cb, own_target // parent_rows, -1)
    row_iota = jnp.arange(rows, dtype=I32)
    same = (owner[:, None] == owner[None, :]) & (row_iota[None, :] < row_iota[:, None])
    place = jnp.where(own_cb, owner * cap + jnp.sum(same.astype(I32), axis=1), -1)

    factors, outgoing = eliminate(
        own_cb[:, None].astype(I32), place[None, :], rank, inv, inv_rel, front_rows, line, file
    )
    received = lax.all_to_all(outgoing, ("front", "helper"), split_axis=0, concat_axis=0, tiled=True)

    below, counts = columns_below(child_map, parent_width)
    source = jnp.where(counts > 0, below, -1.0).astype(I32).reshape(fronts, parent_width)
    group = below[:, :, 0].astype(I32) >> 7

    own_parent = me * parent_rows + jnp.arange(parent_rows, dtype=I32)
    column = jnp.sum(
        jnp.where(child_map[:, None, :] == own_parent[None, :, None], column_iota + 1, 0), axis=2
    )
    found = column > 0
    stored = jnp.sum(
        jnp.where(
            row_list[:, None, :] == (column + (PIVOTS - 1))[:, :, None],
            jnp.arange(row_list.shape[1], dtype=I32),
            0,
        ),
        axis=2,
    )
    sender = stored // rows
    ahead = jnp.sum(
        (
            found[:, None, :]
            & (sender[:, :, None] == sender[:, None, :])
            & (stored[:, None, :] < stored[:, :, None])
        ).astype(I32),
        axis=2,
    )
    front_iota = jnp.arange(fronts, dtype=I32)
    slot = jnp.where(found, (front_iota[:, None] * helpers + sender) * cap + ahead, -1)
    put = jnp.any(slot[:, :, None] == jnp.arange(devices * cap, dtype=I32), axis=0).astype(BF16)
    assembled = assemble(group, source, put, received, parent)
    return (factors[None], assembled)


def solution(mesh):
    in_specs = (P("front", "helper", None), P(), P(), P(("front", "helper"), None))
    out_specs = (P("front", "helper", None), P(("front", "helper"), None))
    return jax.shard_map(local, mesh=mesh, in_specs=in_specs, out_specs=out_specs, check_vma=False)
```

time: 257 us -> 182 us (0.71)
  blocking collectives: 23.1 us -> 0 us
  Pallas kernels: 94.3 us -> 71.4 us
  local copies, waits for them, and re-layouts: 27.7 us -> 7.47 us
  waiting for transfers between devices: 53.1 us -> 44.8 us
  starting transfers between devices: 37.8 us -> 41.5 us
  matrix products: 10.6 us -> 6.98 us
    all_gather x1 -> x0, blocking collectives: 23.1 us -> none  [local(): piv = lax.all_gather(pivot, 'helper', axis=0, tiled=True)]
    pallas_call x1, Pallas kernels: 25 us -> 11.7 us  [assemble(): pl.pallas_call(assemble_kernel, grid_spec=pltpu.PrefetchScalarGridSpec(nu...]
    pallas_call x1, Pallas kernels: 28.3 us -> 15.7 us  [invert(): pl.pallas_call(inverse_kernel, out_shape=(jax.ShapeDtypeStruct((PIVOTS, P...]
    reshape x3 -> x1, local copies, waits for them, and re-layouts: 11.9 us -> 0.68 us  [local(): slot_row, slot_rel = (slot_row.reshape(1, -1), slot_rel.reshape(1, -1))]
    all_to_all x1 -> x2, waiting for transfers between devices: 45.2 us -> 38.7 us  [the longest x1 37.1 us: local(): lax.all_to_all(outgoing, ('front', 'helper'), split_axis=0, concat_axis=0...]
    unnamed x28 -> x40, local copies, waits for them, and re-layouts: 6.69 us -> 2.27 us
    pallas_call x1 -> x3, Pallas kernels: 36.1 us -> 39.9 us  [the longest x1 33.3 us: eliminate(): pl.pallas_call(eliminate_kernel, in_specs=[vmem] * 4 + [hbm] * 18, out_sp...]
    ppermute x16 -> x18, starting transfers between devices: 20.6 us -> 24.2 us  [shift(): return lax.ppermute(value, 'helper', shift_pairs(step))]
  transfers between devices with their start and end apart: 17 -> 20, of which waited for: 3 -> 5; matrix products, arithmetic and copies ran while one was open for 12% -> 11% of each run, Pallas kernels for 11% -> 11%
where the time goes in v2:
time: 182 us
  Pallas kernels  71.4 us (39%)
  waiting for transfers between devices  44.8 us (25%)
  starting transfers between devices  41.5 us (23%)
  other arithmetic  8.51 us (5%)
  local copies, waits for them, and re-layouts  7.47 us (4%)
  matrix products  6.98 us (4%)
    all_to_all x1, waiting for transfers between devices, local(): lax.all_to_all(outgoing, ('front', 'helper'), split_axis=0, concat_axis=0...  37.1 us
    pallas_call x1, Pallas kernels, eliminate(): pl.pallas_call(eliminate_kernel, in_specs=[vmem] * 4 + [hbm] * 18, out_sp...  33.3 us
    ppermute x18, starting transfers between devices, shift(): return lax.ppermute(value, 'helper', shift_pairs(step))  24.2 us
    pallas_call x1, Pallas kernels, invert(): pl.pallas_call(inverse_kernel, out_shape=(jax.ShapeDtypeStruct((PIVOTS, P...  15.7 us
    all_to_all x1, starting transfers between devices, local(): lax.all_to_all(outgoing, ('front', 'helper'), split_axis=0, concat_axis=0...  13.7 us
    pallas_call x1, Pallas kernels, assemble(): pl.pallas_call(assemble_kernel, grid_spec=pltpu.PrefetchScalarGridSpec(nu...  11.7 us
    dot_general x1, matrix products, columns_below(): jnp.einsum('fah,fal->fhl', in_high, in_low, preferred_element_type=F32)  6.54 us
    ppermute x18, waiting for transfers between devices, shift(): return lax.ppermute(value, 'helper', shift_pairs(step))  6.05 us
  transfers between devices with their start and end apart: 20, of which 5 were waited for; matrix products, arithmetic and copies ran while one was open for 11% of the time, Pallas kernels for 11%

profile of v2, /device:TPU:1, one launch (start us, length us, event | category | flops | bytes accessed | tf_op | source)
XLA Modules:
  0.0 181.7 jit_solution(5706502546529234491)
XLA Ops:
  0.7 1.0 compare_reduce_fusion
  2.3 4.1 %shard_map.68 = (f32[24,256]{1,0:T(8,128)}, f32[24,1920]{1,0:T(8,128)}, f32[24,1920]{1,0:T(8,128)}) custom-call(s32[1,256]{1,0:T(1,128)} %get-tuple-element.85.ids_ref, f32[256,4096]{1,0:T(8,128)} %bitcast.14), custom_call_target="tpu_custom_call" | custom-call | tf_op jit(solution)/shard_map/pallas_call | solution.py:68
  6.3 2.0 %collective-permute-start = (f32[24,1920]{1,0:T(8,128)}, f32[24,1920]{1,0:T(8,128)S(1)}, u32[]{:S(2)}, u32[]{:S(2)}) collective-permute-start(f32[24,1920]{1,0:T(8,128)} %get-tuple-element.32.refs_0_), channel_id=1, source_target_pairs={{0,4},{1,5},{2,6},{3,7},{4,8},{5,9},{6,10},{7,11},{8,12},{9,13},{1... | collective-permute-start | bytes 552968 | tf_op jit(solution)/shard_map/ppermute | solution.py:88
  8.4 1.3 collective-permute-start.1
  9.7 1.7 collective-permute-start.2
  11.4 1.3 collective-permute-start.3
  12.7 1.4 collective-permute-start.4
  15.7 1.7 collective-permute-start.5
  18.8 4.0 %shard_map.69.rank_hbm = s32[3840,128]{1,0:T(8,128)} custom-call(s32[1,3840]{1,0:T(1,128)} %get-tuple-element.87.map_ref), custom_call_target="tpu_custom_call" | custom-call | tf_op jit(solution)/shard_map/pallas_call | solution.py:130
  24.3 2.6 %shard_map.70 = (f32[48,1920]{1,0:T(8,128)}, f32[48,1920]{1,0:T(8,128)}, f32[48,1920]{1,0:T(8,128)}, f32[48,1920]{1,0:T(8,128)}) custom-call(f32[24,1920]{1,0:T(8,128)} %get-tuple-element.32.refs_0_, f32[24,1920]{1,0:T(8,128)} %copy-done.11, f32[24,1920]{1,0:T(8,128)} %copy-done.12, f32[24,1920]{1,0:T(8,128)} %copy-done.13, ...), custom_call_target="tpu_custom_call" | custom-call | tf_op jit(solution)/shard_map/pallas_call | solution.py:99
  27.4 2.2 %collective-permute-start.7 = (f32[48,1920]{1,0:T(8,128)}, f32[48,1920]{1,0:T(8,128)S(1)}, u32[]{:S(2)}, u32[]{:S(2)}) collective-permute-start(f32[48,1920]{1,0:T(8,128)} %get-tuple-element.41.refs_1_), channel_id=1, source_target_pairs={{0,3},{1,0},{2,1},{3,2},{4,7},{5,4},{6,5},{7,6},{8,11},{9,8},{10,9... | collective-permute-start | bytes 1105928 | tf_op jit(solution)/shard_map/ppermute | solution.py:88
  29.6 1.5 broadcast_in_dim.160
  31.1 3.6 %all-to-all-start = ((f32[16,24,256]{2,1,0:T(8,128)}), f32[16,24,256]{2,1,0:T(8,128)S(1)}, u32[]{:S(2)}, u32[]{:S(2)}) async-start(f32[16,24,256]{2,1,0:T(8,128)} %broadcast_in_dim.160), calls=%async_computation | async-start | bytes 786432 | tf_op jit(solution)/shard_map/all_to_all | solution.py:433
  35.3 1.3 collective-permute-start.10
  36.6 1.4 collective-permute-start.11
  38.1 2.5 %collective-permute-start.9 = (f32[48,1920]{1,0:T(8,128)}, f32[48,1920]{1,0:T(8,128)S(1)}, u32[]{:S(2)}, u32[]{:S(2)}) collective-permute-start(f32[48,1920]{1,0:T(8,128)} %get-tuple-element.43.refs_9_), channel_id=1, source_target_pairs={{0,12},{1,13},{2,14},{3,15},{4,0},{5,1},{6,2},{7,3},{8,4},{9,5},{1... | collective-permute-start | bytes 1105928 | tf_op jit(solution)/shard_map/ppermute | solution.py:88
  41.0 1.6 all-to-all-done
  43.3 15.7 %shard_map.71 = (f32[256,256]{1,0:T(8,128)}, f32[256,384]{1,0:T(8,128)}) custom-call(s32[1,384]{1,0:T(1,128)} %sub.28.slot_abs_ref, s32[1,384]{1,0:T(1,128)} %reshape.190.slot_rel_ref, f32[384,256]{1,0:T(8,128)} %bitcast.16), custom_call_target="tpu_custom_call" | custom-call | tf_op jit(solution)/shard_map/pallas_call | solution.py:185
  59.1 1.1 collective-permute-start.15
  60.4 2.5 %collective-permute-start.13 = (f32[48,1920]{1,0:T(8,128)S(1)}, f32[48,1920]{1,0:T(8,128)}, u32[]{:S(2)}, u32[]{:S(2)}) collective-permute-start(f32[48,1920]{1,0:T(8,128)S(1)} %collective-permute-done.7.refs_5_), channel_id=1, source_target_pairs={{0,3},{1,0},{2,1},{3,2},{4,7},{5,4},{6,5},{7,6},{8,11},{9,8},{10,9... | collective-permute-start | bytes 1105928 | tf_op jit(solution)/shard_map/ppermute | solution.py:88
  63.2 2.3 %collective-permute-start.17 = (f32[48,1920]{1,0:T(8,128)S(1)}, f32[48,1920]{1,0:T(8,128)}, u32[]{:S(2)}, u32[]{:S(2)}) collective-permute-start(f32[48,1920]{1,0:T(8,128)S(1)} %collective-permute-done.9.refs_13_), channel_id=1, source_target_pairs={{0,12},{1,13},{2,14},{3,15},{4,0},{5,1},{6,2},{7,3},{8,4},{9,5},{1... | collective-permute-start | bytes 1105928 | tf_op jit(solution)/shard_map/ppermute | solution.py:88
  65.6 0.8 copy.18.active_ref
  67.8 3.0 %collective-permute-done.16.refs_14_ = f32[48,1920]{1,0:T(8,128)} collective-permute-done((f32[48,1920]{1,0:T(8,128)S(1)}, f32[48,1920]{1,0:T(8,128)}, u32[]{:S(2)}, u32[]{:S(2)}) %collective-permute-start.16) | collective-permute-done | bytes 368672 | tf_op jit(solution)/shard_map/ppermute | solution.py:88
  70.8 2.4 %collective-permute-done.17.refs_15_ = f32[48,1920]{1,0:T(8,128)} collective-permute-done((f32[48,1920]{1,0:T(8,128)S(1)}, f32[48,1920]{1,0:T(8,128)}, u32[]{:S(2)}, u32[]{:S(2)}) %collective-permute-start.17) | collective-permute-done | bytes 368672 | tf_op jit(solution)/shard_map/ppermute | solution.py:88
  73.2 33.3 %shard_map.72 = (f32[256,4096]{1,0:T(8,128)}, f32[128,2,3840]{2,1,0:T(2,128)}) custom-call(s32[256,1]{1,0:T(8,128)} %copy.18.active_ref, s32[1,256]{1,0:T(1,128)} %bitcast.18, f32[256,256]{1,0:T(8,128)} %get-tuple-element.49.inv_ref, f32[256,384]{1,0:T(8,128)} %get-tuple-element.50.inv_rel_ref, s32[3840,128]{1,0:T(8,128)} %shard_map.69.rank_hbm, ...), custom_call_target="tpu_custom_call" | custom-call | tf_op jit(solution)/shard_map/pallas_call | solution.py:318
  106.6 13.7 %all-to-all-start.1 = ((f32[128,2,3840]{2,1,0:T(2,128)}), f32[128,2,3840]{2,1,0:T(2,128)}, u32[]{:S(2)}, u32[]{:S(2)}) async-start(f32[128,2,3840]{2,1,0:T(2,128)} %get-tuple-element.57), calls=%async_computation.1 | async-start | bytes 7864320 | tf_op jit(solution)/shard_map/all_to_all | solution.py:481
  120.3 1.0 select_reduce_fusion.1
  121.3 1.2 select_reduce_fusion
  123.9 6.5 %fusion.21 = (bf16[8,64]{1,0:T(8,128)(2,1)S(1)}, f32[8,64,128]{2,1,0:T(8,128)S(1)}) fusion(s32[8,3840]{1,0:T(8,128)S(1)} %get-tuple-element.89, s32[8,3840]{1,0:T(8,128)S(1)} %get-tuple-element.88), kind=kOutput, calls=%fused_computation.74 | convolution fusion | flops 509279744 | bytes 508928 | tf_op jit(solution)/shard_map/fah,fal->fhl/dot_general | solution.py:399
  131.3 0.9 copy.21
  132.8 37.1 %all-to-all-done.1.received_ref = f32[128,2,3840]{2,1,0:T(2,128)} async-done(((f32[128,2,3840]{2,1,0:T(2,128)}), f32[128,2,3840]{2,1,0:T(2,128)}, u32[]{:S(2)}, u32[]{:S(2)}) %all-to-all-start.1) | async-done | bytes 3932192 | tf_op jit(solution)/shard_map/all_to_all | solution.py:481
  169.9 11.7 %shard_map.73 = f32[64,8192]{1,0:T(8,128)} custom-call(s32[8,64]{1,0:T(8,128)} %fusion.13.group_ref, s32[8,8192]{1,0:T(8,128)} %bitcast.17, bf16[64,256]{1,0:T(8,128)(2,1)} %convert_element_type.45.put_ref, f32[128,2,3840]{2,1,0:T(2,128)} %all-to-all-done.1.received_ref, f32[64,8192]{1,0:T(8,128)} %parent_ref.1), custom_call_target="tpu_custom_call" | custom-call | tf_op jit(solution)/shard_map/pallas_call | solution.py:376
  (99 shorter events, 11.9 us)
Async XLA Ops:
  0.6 13.6 %copy-start.19 = (s32[4]{0:T(128)S(1)}, s32[4]{0:T(128)}, u32[]{:S(2)}) copy-start(s32[4]{0:T(128)} %constant.137.clone) | copy-start | bytes 52
  0.6 17.6 %copy-start.1 = (s32[8,3840]{1,0:T(8,128)S(1)}, s32[8,3840]{1,0:T(8,128)}, u32[]{:S(2)}) copy-start(s32[8,3840]{1,0:T(8,128)} %param.7) | copy-start | bytes 368644
  2.3 32.4 %copy-start.18 = (s32[1,256]{1,0:T(1,128)S(1)}, s32[1,256]{1,0:T(1,128)}, u32[]{:S(2)}) copy-start(s32[1,256]{1,0:T(1,128)} %get-tuple-element.85.ids_ref) | copy-start | bytes 3076
  6.3 9.3 %collective-permute-start = (f32[24,1920]{1,0:T(8,128)}, f32[24,1920]{1,0:T(8,128)S(1)}, u32[]{:S(2)}, u32[]{:S(2)}) collective-permute-start(f32[24,1920]{1,0:T(8,128)} %get-tuple-element.32.refs_0_), channel_id=1, source_target_pairs={{0,4},{1,5},{2,6},{3,7},{4,8},{5,9},{6,10},{7,11},{8,12},{9,13},{1... | collective-permute-start | bytes 552968 | tf_op jit(solution)/shard_map/ppermute | solution.py:88
  8.4 14.4 %collective-permute-start.1 = (f32[24,1920]{1,0:T(8,128)}, f32[24,1920]{1,0:T(8,128)S(1)}, u32[]{:S(2)}, u32[]{:S(2)}) collective-permute-start(f32[24,1920]{1,0:T(8,128)} %get-tuple-element.32.refs_0_), channel_id=1, source_target_pairs={{0,12},{1,13},{2,14},{3,15},{4,0},{5,1},{6,2},{7,3},{8,4},{9,5},{1... | collective-permute-start | bytes 552968 | tf_op jit(solution)/shard_map/ppermute | solution.py:88
  9.7 13.1 %collective-permute-start.2 = (f32[24,1920]{1,0:T(8,128)}, f32[24,1920]{1,0:T(8,128)S(1)}, u32[]{:S(2)}, u32[]{:S(2)}) collective-permute-start(f32[24,1920]{1,0:T(8,128)} %get-tuple-element.32.refs_0_), channel_id=1, source_target_pairs={{0,8},{1,9},{2,10},{3,11},{4,12},{5,13},{6,14},{7,15},{8,0},{9,1},... | collective-permute-start | bytes 552968 | tf_op jit(solution)/shard_map/ppermute | solution.py:88
  11.4 11.4 %collective-permute-start.3 = (f32[24,1920]{1,0:T(8,128)}, f32[24,1920]{1,0:T(8,128)S(1)}, u32[]{:S(2)}, u32[]{:S(2)}) collective-permute-start(f32[24,1920]{1,0:T(8,128)} %get-tuple-element.36.refs_4_), channel_id=1, source_target_pairs={{0,1},{1,2},{2,3},{3,0},{4,5},{5,6},{6,7},{7,4},{8,9},{9,10},{10,1... | collective-permute-start | bytes 552968 | tf_op jit(solution)/shard_map/ppermute | solution.py:88
  12.7 10.2 %collective-permute-start.4 = (f32[24,1920]{1,0:T(8,128)}, f32[24,1920]{1,0:T(8,128)S(1)}, u32[]{:S(2)}, u32[]{:S(2)}) collective-permute-start(f32[24,1920]{1,0:T(8,128)} %get-tuple-element.36.refs_4_), channel_id=1, source_target_pairs={{0,3},{1,0},{2,1},{3,2},{4,7},{5,4},{6,5},{7,6},{8,11},{9,8},{10,9... | collective-permute-start | bytes 552968 | tf_op jit(solution)/shard_map/ppermute | solution.py:88
  15.7 7.2 %copy-start.11 = (f32[24,1920]{1,0:T(8,128)}, f32[24,1920]{1,0:T(8,128)S(1)}, u32[]{:S(2)}) copy-start(f32[24,1920]{1,0:T(8,128)S(1)} %collective-permute-done.refs_1_) | copy-start | bytes 552964
  15.7 7.2 %collective-permute-start.5 = (f32[24,1920]{1,0:T(8,128)}, f32[24,1920]{1,0:T(8,128)S(1)}, u32[]{:S(2)}, u32[]{:S(2)}) collective-permute-start(f32[24,1920]{1,0:T(8,128)} %get-tuple-element.36.refs_4_), channel_id=1, source_target_pairs={{0,2},{1,3},{2,0},{3,1},{4,6},{5,7},{6,4},{7,5},{8,10},{9,11},{10,... | collective-permute-start | bytes 552968 | tf_op jit(solution)/shard_map/ppermute | solution.py:88
  26.9 13.7 %collective-permute-start.6 = (f32[48,1920]{1,0:T(8,128)}, f32[48,1920]{1,0:T(8,128)S(1)}, u32[]{:S(2)}, u32[]{:S(2)}) collective-permute-start(f32[48,1920]{1,0:T(8,128)} %get-tuple-element.40.refs_0_), channel_id=1, source_target_pairs={{0,1},{1,2},{2,3},{3,0},{4,5},{5,6},{6,7},{7,4},{8,9},{9,10},{10,1... | collective-permute-start | bytes 1105928 | tf_op jit(solution)/shard_map/ppermute | solution.py:88
  27.4 13.3 %collective-permute-start.7 = (f32[48,1920]{1,0:T(8,128)}, f32[48,1920]{1,0:T(8,128)S(1)}, u32[]{:S(2)}, u32[]{:S(2)}) collective-permute-start(f32[48,1920]{1,0:T(8,128)} %get-tuple-element.41.refs_1_), channel_id=1, source_target_pairs={{0,3},{1,0},{2,1},{3,2},{4,7},{5,4},{6,5},{7,6},{8,11},{9,8},{10,9... | collective-permute-start | bytes 1105928 | tf_op jit(solution)/shard_map/ppermute | solution.py:88
  31.1 11.5 %all-to-all-start = ((f32[16,24,256]{2,1,0:T(8,128)}), f32[16,24,256]{2,1,0:T(8,128)S(1)}, u32[]{:S(2)}, u32[]{:S(2)}) async-start(f32[16,24,256]{2,1,0:T(8,128)} %broadcast_in_dim.160), calls=%async_computation | async-start | bytes 786432 | tf_op jit(solution)/shard_map/all_to_all | solution.py:433
  35.3 25.1 %collective-permute-start.10 = (f32[48,1920]{1,0:T(8,128)}, f32[48,1920]{1,0:T(8,128)S(1)}, u32[]{:S(2)}, u32[]{:S(2)}) collective-permute-start(f32[48,1920]{1,0:T(8,128)} %get-tuple-element.41.refs_1_), channel_id=1, source_target_pairs={{0,1},{1,2},{2,3},{3,0},{4,5},{5,6},{6,7},{7,4},{8,9},{9,10},{10,1... | collective-permute-start | bytes 1105928 | tf_op jit(solution)/shard_map/ppermute | solution.py:88
  36.6 26.3 %collective-permute-start.11 = (f32[48,1920]{1,0:T(8,128)}, f32[48,1920]{1,0:T(8,128)S(1)}, u32[]{:S(2)}, u32[]{:S(2)}) collective-permute-start(f32[48,1920]{1,0:T(8,128)} %get-tuple-element.40.refs_0_), channel_id=1, source_target_pairs={{0,3},{1,0},{2,1},{3,2},{4,7},{5,4},{6,5},{7,6},{8,11},{9,8},{10,9... | collective-permute-start | bytes 1105928 | tf_op jit(solution)/shard_map/ppermute | solution.py:88
  38.1 22.1 %collective-permute-start.9 = (f32[48,1920]{1,0:T(8,128)}, f32[48,1920]{1,0:T(8,128)S(1)}, u32[]{:S(2)}, u32[]{:S(2)}) collective-permute-start(f32[48,1920]{1,0:T(8,128)} %get-tuple-element.43.refs_9_), channel_id=1, source_target_pairs={{0,12},{1,13},{2,14},{3,15},{4,0},{5,1},{6,2},{7,3},{8,4},{9,5},{1... | collective-permute-start | bytes 1105928 | tf_op jit(solution)/shard_map/ppermute | solution.py:88
  40.6 32.5 %copy-start.2 = (f32[48,1920]{1,0:T(8,128)}, f32[48,1920]{1,0:T(8,128)S(1)}, u32[]{:S(2)}) copy-start(f32[48,1920]{1,0:T(8,128)S(1)} %collective-permute-done.6.refs_2_) | copy-start | bytes 1105924
  40.6 22.6 %collective-permute-start.14 = (f32[48,1920]{1,0:T(8,128)}, f32[48,1920]{1,0:T(8,128)S(1)}, u32[]{:S(2)}, u32[]{:S(2)}) collective-permute-start(f32[48,1920]{1,0:T(8,128)} %get-tuple-element.43.refs_9_), channel_id=1, source_target_pairs={{0,4},{1,5},{2,6},{3,7},{4,8},{5,9},{6,10},{7,11},{8,12},{9,13},{1... | collective-permute-start | bytes 1105928 | tf_op jit(solution)/shard_map/ppermute | solution.py:88
  40.6 32.5 %copy-start.3 = (f32[48,1920]{1,0:T(8,128)}, f32[48,1920]{1,0:T(8,128)S(1)}, u32[]{:S(2)}) copy-start(f32[48,1920]{1,0:T(8,128)S(1)} %collective-permute-done.7.refs_5_) | copy-start | bytes 1105924
  40.6 18.4 %collective-permute-start.8 = (f32[48,1920]{1,0:T(8,128)}, f32[48,1920]{1,0:T(8,128)S(1)}, u32[]{:S(2)}, u32[]{:S(2)}) collective-permute-start(f32[48,1920]{1,0:T(8,128)} %get-tuple-element.42.refs_8_), channel_id=1, source_target_pairs={{0,4},{1,5},{2,6},{3,7},{4,8},{5,9},{6,10},{7,11},{8,12},{9,13},{1... | collective-permute-start | bytes 1105928 | tf_op jit(solution)/shard_map/ppermute | solution.py:88
  59.1 14.1 %copy-start.8 = (f32[48,1920]{1,0:T(8,128)}, f32[48,1920]{1,0:T(8,128)S(1)}, u32[]{:S(2)}) copy-start(f32[48,1920]{1,0:T(8,128)S(1)} %collective-permute-done.8.refs_10_) | copy-start | bytes 1105924
  59.1 8.1 %collective-permute-start.15 = (f32[48,1920]{1,0:T(8,128)}, f32[48,1920]{1,0:T(8,128)S(1)}, u32[]{:S(2)}, u32[]{:S(2)}) collective-permute-start(f32[48,1920]{1,0:T(8,128)} %get-tuple-element.42.refs_8_), channel_id=1, source_target_pairs={{0,12},{1,13},{2,14},{3,15},{4,0},{5,1},{6,2},{7,3},{8,4},{9,5},{1... | collective-permute-start | bytes 1105928 | tf_op jit(solution)/shard_map/ppermute | solution.py:88
  60.2 12.9 %copy-start.6 = (f32[48,1920]{1,0:T(8,128)}, f32[48,1920]{1,0:T(8,128)S(1)}, u32[]{:S(2)}) copy-start(f32[48,1920]{1,0:T(8,128)S(1)} %collective-permute-done.9.refs_13_) | copy-start | bytes 1105924
  60.2 7.6 %collective-permute-start.12 = (f32[48,1920]{1,0:T(8,128)S(1)}, f32[48,1920]{1,0:T(8,128)S(1)}, u32[]{:S(2)}, u32[]{:S(2)}) collective-permute-start(f32[48,1920]{1,0:T(8,128)S(1)} %collective-permute-done.6.refs_2_), channel_id=1, source_target_pairs={{0,1},{1,2},{2,3},{3,0},{4,5},{5,6},{6,7},{7,4},{8,9},{9,10},{10,1... | collective-permute-start | bytes 1105928 | tf_op jit(solution)/shard_map/ppermute | solution.py:88
  60.4 12.7 %copy-start.4 = (f32[48,1920]{1,0:T(8,128)}, f32[48,1920]{1,0:T(8,128)S(1)}, u32[]{:S(2)}) copy-start(f32[48,1920]{1,0:T(8,128)S(1)} %collective-permute-done.10.refs_3_) | copy-start | bytes 1105924
  60.4 7.3 %collective-permute-start.13 = (f32[48,1920]{1,0:T(8,128)S(1)}, f32[48,1920]{1,0:T(8,128)}, u32[]{:S(2)}, u32[]{:S(2)}) collective-permute-start(f32[48,1920]{1,0:T(8,128)S(1)} %collective-permute-done.7.refs_5_), channel_id=1, source_target_pairs={{0,3},{1,0},{2,1},{3,2},{4,7},{5,4},{6,5},{7,6},{8,11},{9,8},{10,9... | collective-permute-start | bytes 1105928 | tf_op jit(solution)/shard_map/ppermute | solution.py:88
  62.9 10.3 %copy-start.5 = (f32[48,1920]{1,0:T(8,128)}, f32[48,1920]{1,0:T(8,128)S(1)}, u32[]{:S(2)}) copy-start(f32[48,1920]{1,0:T(8,128)S(1)} %collective-permute-done.11.refs_4_) | copy-start | bytes 1105924
  62.9 7.9 %collective-permute-start.16 = (f32[48,1920]{1,0:T(8,128)S(1)}, f32[48,1920]{1,0:T(8,128)}, u32[]{:S(2)}, u32[]{:S(2)}) collective-permute-start(f32[48,1920]{1,0:T(8,128)S(1)} %collective-permute-done.8.refs_10_), channel_id=1, source_target_pairs={{0,4},{1,5},{2,6},{3,7},{4,8},{5,9},{6,10},{7,11},{8,12},{9,13},{1... | collective-permute-start | bytes 1105928 | tf_op jit(solution)/shard_map/ppermute | solution.py:88
  63.2 9.9 %copy-start.7 = (f32[48,1920]{1,0:T(8,128)}, f32[48,1920]{1,0:T(8,128)S(1)}, u32[]{:S(2)}) copy-start(f32[48,1920]{1,0:T(8,128)S(1)} %collective-permute-done.14.refs_11_) | copy-start | bytes 1105924
  63.2 9.9 %collective-permute-start.17 = (f32[48,1920]{1,0:T(8,128)S(1)}, f32[48,1920]{1,0:T(8,128)}, u32[]{:S(2)}, u32[]{:S(2)}) collective-permute-start(f32[48,1920]{1,0:T(8,128)S(1)} %collective-permute-done.9.refs_13_), channel_id=1, source_target_pairs={{0,12},{1,13},{2,14},{3,15},{4,0},{5,1},{6,2},{7,3},{8,4},{9,5},{1... | collective-permute-start | bytes 1105928 | tf_op jit(solution)/shard_map/ppermute | solution.py:88
  106.6 14.8 %copy-start.17 = (s32[8,4096]{1,0:T(8,128)S(1)}, s32[8,4096]{1,0:T(8,128)}, u32[]{:S(2)}) copy-start(s32[8,4096]{1,0:T(8,128)} %param.6) | copy-start | bytes 393220
  106.6 63.4 %all-to-all-start.1 = ((f32[128,2,3840]{2,1,0:T(2,128)}), f32[128,2,3840]{2,1,0:T(2,128)}, u32[]{:S(2)}, u32[]{:S(2)}) async-start(f32[128,2,3840]{2,1,0:T(2,128)} %get-tuple-element.57), calls=%async_computation.1 | async-start | bytes 7864320 | tf_op jit(solution)/shard_map/all_to_all | solution.py:481
  (8 other events, 15.9 us)

commit v3 on v2

--- a/solution.py
+++ b/solution.py
@@ -58,7 +58,11 @@
             middle, low = halves(value - high.astype(F32))
             into[:, at:stop] = dot16(chosen, high) + (dot16(chosen, middle) + dot16(chosen, low))
 
-    pick(0, pivot_ref)
+    high = front_ref[:, :PIVOTS].astype(BF16)
+    middle, low = halves(front_ref[:, :PIVOTS] - high.astype(F32))
+    pivot = dot16(chosen, high) + (dot16(chosen, middle) + dot16(chosen, low))
+    for helper in range(pivot_ref.shape[0]):
+        pivot_ref[helper] = pivot
     pick(PIVOTS, first_ref)
     pick(PIVOTS + first_ref.shape[1], second_ref)
 
@@ -68,7 +72,7 @@
     return pl.pallas_call(
         select_kernel,
         out_shape=(
-            jax.ShapeDtypeStruct((CAP, PIVOTS), F32),
+            jax.ShapeDtypeStruct((GRID * GRID, CAP, PIVOTS), F32),
             jax.ShapeDtypeStruct((CAP, half), F32),
             jax.ShapeDtypeStruct((CAP, half), F32),
         ),
@@ -90,17 +94,35 @@
 
 def pack_kernel(*refs):
     for index in range(8):
-        into = slice(index % 2 * CAP, (index % 2 + 1) * CAP)
-        refs[8 + index // 2][into, :] = refs[index][...]
+        into = slice(index % 4 * CAP, (index % 4 + 1) * CAP)
+        refs[8 + index // 4][into, :] = refs[index][...]
 
 
 def pack(firsts, seconds):
     half = seconds[0].shape[1]
     return pl.pallas_call(
         pack_kernel,
-        out_shape=(jax.ShapeDtypeStruct((2 * CAP, half), F32),) * 4,
+        out_shape=(jax.ShapeDtypeStruct((4 * CAP, half), F32),) * 2,
         compiler_params=BIG,
     )(*firsts, *seconds)
+
+
+def cut_kernel(*refs):
+    for index in range(4):
+        refs[4 + index][...] = refs[index][...]
+
+
+def cut(*blocks):
+    rows, width = blocks[0].shape
+    half = (rows // 2, width)
+    return pl.pallas_call(
+        cut_kernel,
+        grid=(1,),
+        in_specs=[pl.BlockSpec(half, lambda i: (0, 0)), pl.BlockSpec(half, lambda i: (1, 0))] * 2,
+        out_specs=[pl.BlockSpec(half, lambda i: (0, 0))] * 4,
+        out_shape=(jax.ShapeDtypeStruct(half, F32),) * 4,
+        compiler_params=BIG,
+    )(*blocks)
 
 
 def rank_kernel(map_ref, rank_ref):
@@ -195,24 +217,54 @@
 OFFSETS = (0, 3, 1, 2)
 
 
+def lower_kernel(active_ref, inv_ref, inv_rel_ref, current_ref, first_ref, lower_ref):
+    active = active_ref[...] > 0
+    current = current_ref[...]
+    first_ref[...] = jnp.where(active, dot3(current, inv_ref[...]), current)
+    high, low = halves(jnp.where(active, dot3(current, inv_rel_ref[...]), 0.0))
+    slots = high.shape[1]
+    lower_ref[:, :slots] = high
+    lower_ref[:, slots : 2 * slots] = high
+    lower_ref[:, 2 * slots :] = low
+
+
+def lower_factor(active, inv, inv_rel, front_rows):
+    rows = front_rows.shape[0]
+    slots = inv_rel.shape[1]
+    whole = lambda shape: pl.BlockSpec(shape, lambda i: (0, 0))
+    return pl.pallas_call(
+        lower_kernel,
+        grid=(1,),
+        in_specs=[whole(active.shape), whole(inv.shape), whole(inv_rel.shape), whole((rows, PIVOTS))],
+        out_specs=[whole((rows, PIVOTS)), whole((rows, 3 * slots))],
+        out_shape=(
+            jax.ShapeDtypeStruct((rows, PIVOTS), F32),
+            jax.ShapeDtypeStruct((rows, 3 * slots), BF16),
+        ),
+        compiler_params=BIG,
+    )(active, inv, inv_rel, front_rows)
+
+
 def eliminate_kernel(
-    active_ref, place_ref, inv_ref, inv_rel_ref, rank_hbm, front_hbm, *refs
+    place_ref, first_ref, lower_ref, rank_hbm, front_hbm, *refs
 ):
-    pieces, refs = refs[:16], refs[16:]
+    pieces, refs = refs[:10], refs[10:]
     factors_hbm, send_hbm = refs[:2]
     matrix, upper, ranks, sorted_in, moves, send = refs[2:8]
     front_sem, upper_sem, rank_sem, factors_sem, send_sem = refs[8:]
-    rows, columns = matrix.shape
-    width = columns - PIVOTS
+    rows, width = matrix.shape
     half = width // 2
+    slots = upper.shape[0]
     tile = 256
     tiles = width // tile
 
-    loads = [pltpu.make_async_copy(front_hbm.at[:, :PIVOTS], matrix.at[:, :PIVOTS], front_sem.at[0])]
+    loads = []
     for part in range(2):
-        at = PIVOTS + part * half
+        at = part * half
         loads.append(
-            pltpu.make_async_copy(front_hbm.at[:, at : at + half], matrix.at[:, at : at + half], front_sem.at[part + 1])
+            pltpu.make_async_copy(
+                front_hbm.at[:, PIVOTS + at : PIVOTS + at + half], matrix.at[:, at : at + half], front_sem.at[part]
+            )
         )
     rank_load = pltpu.make_async_copy(rank_hbm, ranks, rank_sem)
     upper_loads = []
@@ -220,43 +272,36 @@
         into = slice(part * half, (part + 1) * half)
         for piece in range(4):
             for block in range(4):
-                source, at = pieces[part * 8 + piece * 2 + block // 2], block % 2 * CAP
+                if piece < 3:
+                    source, at = pieces[part * 5 + piece], block * CAP
+                else:
+                    source, at = pieces[part * 5 + 3 + block // 2], block % 2 * CAP
                 slot = ((block * 4 + piece) if part == 0 else (piece * 4 + block)) * CAP
                 upper_loads.append(
                     pltpu.make_async_copy(
                         source.at[at : at + CAP, :], upper.at[slot : slot + CAP, into], upper_sem.at[part * 16 + piece * 4 + block]
                     )
                 )
-    loads[0].start()
-    loads[1].start()
-    for load in upper_loads[:16]:
-        load.start()
-    loads[2].start()
-    for load in upper_loads[16:]:
-        load.start()
-    rank_load.start()
-
-    loads[0].wait()
-    active = active_ref[...] > 0
-    current = matrix[:, :PIVOTS]
-    lower = jnp.where(active, dot3(current, inv_rel_ref[...]), 0.0)
-    lower_high, lower_low = halves(lower)
-    lower_both = jnp.concatenate([lower_high, lower_low], axis=0)
-    matrix[:, :PIVOTS] = jnp.where(active, dot3(current, inv_ref[...]), current)
-    stores = [pltpu.make_async_copy(matrix.at[:, :PIVOTS], factors_hbm.at[:, :PIVOTS], factors_sem.at[0])]
+    for part in range(2):
+        for load in upper_loads[part * 16 : part * 16 + 16]:
+            load.start()
+        loads[part].start()
+        if part == 0:
+            rank_load.start()
+    stores = [pltpu.make_async_copy(first_ref, factors_hbm.at[:, :PIVOTS], factors_sem.at[0])]
     stores[0].start()
     place = (iota((rows, rows), 0) == place_ref[...]).astype(F32).astype(BF16)
+    lower_high, lower_low = lower_ref[:, : 2 * slots], lower_ref[:, 2 * slots :]
 
     def update(at, size):
-        high, low = halves(upper[:, pl.ds(at, size)])
-        change = dot16(lower_both, high)
-        change = change[:rows] + (change[rows:] + dot16(lower_high, low))
-        out = matrix[:, pl.ds(at + PIVOTS, size)] - change
-        matrix[:, pl.ds(at + PIVOTS, size)] = out
+        high, low = halves(upper[:, at : at + size])
+        change = dot16(lower_high, jnp.concatenate([high, low], axis=0)) + dot16(lower_low, high)
+        out = matrix[:, at : at + size] - change
+        matrix[:, at : at + size] = out
         high, low = halves(out)
         placed = dot16(place, jnp.concatenate([high, low], axis=1)).astype(BF16)
-        sorted_in[:rows, pl.ds(at, size)] = placed[:, :size]
-        sorted_in[rows:, pl.ds(at, size)] = placed[:, size:]
+        sorted_in[:rows, at : at + size] = placed[:, :size]
+        sorted_in[rows:, at : at + size] = placed[:, size:]
 
     def generate(slot, index):
         lane = iota((1, 128), 1) + index * tile
@@ -265,24 +310,33 @@
                 (ranks[...] == lane + part * 128).astype(F32).astype(BF16)
             )
 
-    for part in range(2):
-        loads[part + 1].wait()
+    def ready(part):
+        loads[part].wait()
         for load in upper_loads[part * 16 : part * 16 + 16]:
             load.wait()
 
-        def updates(index, carry):
-            update(pl.multiple_of(part * half + index * 384, 128), 384)
-            return carry
-
-        lax.fori_loop(0, half // 384, updates, 0)
-        at = PIVOTS + part * half
+    def store(part):
+        at = part * half
         stores.append(
-            pltpu.make_async_copy(matrix.at[:, at : at + half], factors_hbm.at[:, at : at + half], factors_sem.at[part + 1])
+            pltpu.make_async_copy(
+                matrix.at[:, at : at + half],
+                factors_hbm.at[:, PIVOTS + at : PIVOTS + at + half],
+                factors_sem.at[part + 1],
+            )
         )
         stores[-1].start()
 
-    rank_load.wait()
-    generate(0, 0)
+    span = 768
+    ready(0)
+    for at in range(0, width, span):
+        if at < half < at + span:
+            rank_load.wait()
+            generate(0, 0)
+            ready(1)
+        update(at, span)
+        if at < half <= at + span:
+            store(0)
+    store(1)
 
     def permute(slot, index):
         at = pl.multiple_of(index * tile, tile)
@@ -310,34 +364,34 @@
         ).wait()
 
 
-def eliminate(active, place, rank, inv, inv_rel, front_rows, line, file):
+def eliminate(place, rank, first, lower, front_rows, line, file):
     rows, columns = front_rows.shape
     width = columns - PIVOTS
     vmem = pl.BlockSpec(memory_space=pltpu.VMEM)
     hbm = pl.BlockSpec(memory_space=pl.ANY)
     return pl.pallas_call(
         eliminate_kernel,
-        in_specs=[vmem] * 4 + [hbm] * 18,
+        in_specs=[vmem] * 3 + [hbm] * 12,
         out_specs=(hbm, hbm),
         out_shape=(
             jax.ShapeDtypeStruct((rows, columns), F32),
             jax.ShapeDtypeStruct((rows // 2, 2, width), F32),
         ),
         scratch_shapes=[
-            pltpu.VMEM((rows, columns), F32),
+            pltpu.VMEM((rows, width), F32),
             pltpu.VMEM((16 * CAP, width), F32),
             pltpu.VMEM(rank.shape, I32),
             pltpu.VMEM((2 * rows, width), BF16),
             pltpu.VMEM((2, width, 256), BF16),
             pltpu.VMEM((rows // 2, 2, width), F32),
-            pltpu.SemaphoreType.DMA((3,)),
+            pltpu.SemaphoreType.DMA((2,)),
             pltpu.SemaphoreType.DMA((32,)),
             pltpu.SemaphoreType.DMA,
             pltpu.SemaphoreType.DMA((3,)),
             pltpu.SemaphoreType.DMA((width // 256,)),
         ],
         compiler_params=BIG,
-    )(active, place, inv, inv_rel, rank, front_rows, *line, *file)
+    )(place, first, lower, rank, front_rows, *line, *file)
 
 
 def assemble_kernel(group_ref, source_ref, put_ref, received_ref, parent_ref, out_ref):
@@ -430,9 +484,8 @@
 
     pivot, first, second = select_panel(own_ids, front_rows)
     own_map = jnp.take(child_map, my_front, axis=0)
-    piv = lax.all_to_all(
-        jnp.broadcast_to(pivot[None], (helpers, CAP, PIVOTS)), "helper", split_axis=0, concat_axis=0, tiled=True
-    ).reshape(helpers * CAP, PIVOTS)
+    piv = lax.all_to_all(pivot, "helper", split_axis=0, concat_axis=0, tiled=True)
+    piv = piv.reshape(helpers * CAP, PIVOTS)
     firsts = (first, shift(first, X_UP), shift(first, X_DOWN), shift(first, X_FAR))
     seconds = (second, shift(second, Y_UP), shift(second, Y_DOWN), shift(second, Y_FAR))
 
@@ -451,19 +504,20 @@
     )
     rank = column_ranks(own_map)
     slot_row, slot_rel = slot_row.reshape(1, -1), slot_rel.reshape(1, -1)
-    firsts, seconds, rank, slot_row, slot_rel = lax.optimization_barrier((firsts, seconds, rank, slot_row, slot_rel))
-
-    line_a, line_b, file_a, file_b = pack(firsts, seconds)
-    line_up, line_down = shift(line_a, Y_UP), shift(line_b, Y_DOWN)
-    file_up, file_down = shift(file_a, X_UP), shift(file_b, X_DOWN)
-    line_rest = shift(line_b, Y_UP), shift(line_a, Y_DOWN)
-    file_rest = shift(file_b, X_UP), shift(file_a, X_DOWN)
+    firsts, seconds, rank, slot_row, slot_rel, piv = lax.optimization_barrier(
+        (firsts, seconds, rank, slot_row, slot_rel, piv)
+    )
+
+    line, file = pack(firsts, seconds)
+    line_up, line_down = shift(line, Y_UP), shift(line, Y_DOWN)
+    file_up, file_down = shift(file, X_UP), shift(file, X_DOWN)
     inv, inv_rel = invert(slot_row, slot_rel, piv)
     line_up, line_down, file_up, file_down, inv, inv_rel = lax.optimization_barrier(
         (line_up, line_down, file_up, file_down, inv, inv_rel)
     )
-    line = (line_a, line_b, line_up, line_rest[0], line_rest[1], line_down, shift(line_up, Y_UP), shift(line_down, Y_DOWN))
-    file = (file_a, file_b, file_up, file_rest[0], file_rest[1], file_down, shift(file_up, X_UP), shift(file_down, X_DOWN))
+    up, down, left, right = cut(line_up, line_down, file_up, file_down)
+    line = (line, line_up, line_down, shift(up, Y_UP), shift(down, Y_DOWN))
+    file = (file, file_up, file_down, shift(left, X_UP), shift(right, X_DOWN))
 
     own_cb = own_ids >= PIVOTS
     column_iota = jnp.arange(width, dtype=I32)
@@ -475,9 +529,8 @@
     same = (owner[:, None] == owner[None, :]) & (row_iota[None, :] < row_iota[:, None])
     place = jnp.where(own_cb, owner * cap + jnp.sum(same.astype(I32), axis=1), -1)
 
-    factors, outgoing = eliminate(
-        own_cb[:, None].astype(I32), place[None, :], rank, inv, inv_rel, front_rows, line, file
-    )
+    first_columns, lower = lower_factor(own_cb[:, None].astype(I32), inv, inv_rel, front_rows)
+    factors, outgoing = eliminate(place[None, :], rank, first_columns, lower, front_rows, line, file)
     received = lax.all_to_all(outgoing, ("front", "helper"), split_axis=0, concat_axis=0, tiled=True)
 
     below, counts = columns_below(child_map, parent_width)

time: 182 us -> 176 us (0.967)
  waiting for transfers between devices: 44.8 us -> 40.4 us
  starting transfers between devices: 41.5 us -> 37.9 us
  Pallas kernels: 71.4 us -> 73.4 us
    ppermute x18 -> x14, starting transfers between devices: 24.2 us -> 21.4 us  [shift(): return lax.ppermute(value, 'helper', shift_pairs(step))]
    ppermute x18 -> x14, waiting for transfers between devices: 6.05 us -> 3.3 us  [shift(): return lax.ppermute(value, 'helper', shift_pairs(step))]
    pallas_call x3 -> x5, Pallas kernels: 40 us -> 42 us  [the longest x1 30.4 us: eliminate(): pl.pallas_call(eliminate_kernel, in_specs=[vmem] * 3 + [hbm] * 12, out_sp...]
  transfers between devices with their start and end apart: 20 -> 16, of which waited for: 5 -> 3; matrix products, arithmetic and copies ran while one was open for 11% -> 10% of each run, Pallas kernels for 11% -> 13%
where the time goes in v3:
time: 176 us; the launch traced here: 175 us
  Pallas kernels  73.4 us (42%)
  waiting for transfers between devices  40.4 us (23%)
  starting transfers between devices  37.9 us (22%)
  other arithmetic  8.58 us (5%)
  matrix products  6.98 us (4%)
  local copies, waits for them, and re-layouts  6.66 us (4%)
    all_to_all x1, waiting for transfers between devices, local(): lax.all_to_all(outgoing, ('front', 'helper'), split_axis=0, concat_axis=0...  37.1 us
    pallas_call x1, Pallas kernels, eliminate(): pl.pallas_call(eliminate_kernel, in_specs=[vmem] * 3 + [hbm] * 12, out_sp...  30.4 us
    ppermute x14, starting transfers between devices, shift(): return lax.ppermute(value, 'helper', shift_pairs(step))  21.4 us
    pallas_call x1, Pallas kernels, invert(): pl.pallas_call(inverse_kernel, out_shape=(jax.ShapeDtypeStruct((PIVOTS, P...  15.7 us
    all_to_all x1, starting transfers between devices, local(): lax.all_to_all(outgoing, ('front', 'helper'), split_axis=0, concat_axis=0...  12.3 us
    pallas_call x1, Pallas kernels, assemble(): pl.pallas_call(assemble_kernel, grid_spec=pltpu.PrefetchScalarGridSpec(nu...  11.7 us
    dot_general x1, matrix products, columns_below(): jnp.einsum('fah,fal->fhl', in_high, in_low, preferred_element_type=F32)  6.54 us
    all_to_all x1, starting transfers between devices, local(): lax.all_to_all(pivot, 'helper', split_axis=0, concat_axis=0, tiled=True)  4.18 us
  transfers between devices with their start and end apart: 16, of which 3 were waited for; matrix products, arithmetic and copies ran while one was open for 10% of the time, Pallas kernels for 13%

profile of v3, /device:TPU:1, one launch (start us, length us, event | category | flops | bytes accessed | tf_op | source)
XLA Modules:
  0.0 175.0 jit_solution(16579246023673917748)
XLA Ops:
  0.7 1.0 compare_reduce_fusion
  2.3 4.1 %shard_map.68 = (f32[16,24,256]{2,1,0:T(8,128)}, f32[24,1920]{1,0:T(8,128)}, f32[24,1920]{1,0:T(8,128)}) custom-call(s32[1,256]{1,0:T(1,128)} %get-tuple-element.95.ids_ref, f32[256,4096]{1,0:T(8,128)} %bitcast.14), custom_call_target="tpu_custom_call" | custom-call | tf_op jit(solution)/shard_map/pallas_call | solution.py:72
  6.4 2.0 %collective-permute-start = (f32[24,1920]{1,0:T(8,128)}, f32[24,1920]{1,0:T(8,128)S(1)}, u32[]{:S(2)}, u32[]{:S(2)}) collective-permute-start(f32[24,1920]{1,0:T(8,128)} %get-tuple-element.38.refs_0_), channel_id=1, source_target_pairs={{0,4},{1,5},{2,6},{3,7},{4,8},{5,9},{6,10},{7,11},{8,12},{9,13},{1... | collective-permute-start | bytes 552968 | tf_op jit(solution)/shard_map/ppermute | solution.py:92
  8.4 1.3 collective-permute-start.1
  9.7 1.7 collective-permute-start.2
  11.4 1.3 collective-permute-start.3
  12.7 1.4 collective-permute-start.4
  14.2 4.2 %all-to-all-start = ((f32[16,24,256]{2,1,0:T(8,128)}), f32[16,24,256]{2,1,0:T(8,128)S(1)}, u32[]{:S(2)}, u32[]{:S(2)}) async-start(f32[16,24,256]{2,1,0:T(8,128)} %get-tuple-element.37), calls=%async_computation | async-start | bytes 786432 | tf_op jit(solution)/shard_map/all_to_all | solution.py:487
  19.9 2.9 %collective-permute-start.5 = (f32[24,1920]{1,0:T(8,128)}, f32[24,1920]{1,0:T(8,128)S(1)}, u32[]{:S(2)}, u32[]{:S(2)}) collective-permute-start(f32[24,1920]{1,0:T(8,128)} %get-tuple-element.42.refs_4_), channel_id=1, source_target_pairs={{0,2},{1,3},{2,0},{3,1},{4,6},{5,7},{6,4},{7,5},{8,10},{9,11},{10,... | collective-permute-start | bytes 552968 | tf_op jit(solution)/shard_map/ppermute | solution.py:92
  24.2 4.0 %shard_map.69.rank_hbm = s32[3840,128]{1,0:T(8,128)} custom-call(s32[1,3840]{1,0:T(1,128)} %get-tuple-element.97.map_ref), custom_call_target="tpu_custom_call" | custom-call | tf_op jit(solution)/shard_map/pallas_call | solution.py:152
  28.3 2.0 %collective-permute-done.5.refs_7_ = f32[24,1920]{1,0:T(8,128)S(1)} collective-permute-done((f32[24,1920]{1,0:T(8,128)}, f32[24,1920]{1,0:T(8,128)S(1)}, u32[]{:S(2)}, u32[]{:S(2)}) %collective-permute-start.5) | collective-permute-done | bytes 184352 | tf_op jit(solution)/shard_map/ppermute | solution.py:92
  31.0 2.6 %shard_map.70 = (f32[96,1920]{1,0:T(8,128)}, f32[96,1920]{1,0:T(8,128)}) custom-call(f32[24,1920]{1,0:T(8,128)} %get-tuple-element.38.refs_0_, f32[24,1920]{1,0:T(8,128)} %copy-done.10, f32[24,1920]{1,0:T(8,128)} %copy-done.11, f32[24,1920]{1,0:T(8,128)} %copy-done.12, f32[24,1920]{1,0:T(8,128)} %get-tuple-element.42.refs_4_, f32[24,1920]{1,0:T(8,128)} %copy-done.13, ...), custom_call_target="tpu_custom_call" | custom-call | tf_op jit(solution)/shard_map/pallas_call | solution.py:103
  33.5 1.8 %collective-permute-start.6 = (f32[96,1920]{1,0:T(8,128)}, f32[96,1920]{1,0:T(8,128)S(1)}, u32[]{:S(2)}, u32[]{:S(2)}) collective-permute-start(f32[96,1920]{1,0:T(8,128)} %get-tuple-element.46.refs_0_), channel_id=1, source_target_pairs={{0,1},{1,2},{2,3},{3,0},{4,5},{5,6},{6,7},{7,4},{8,9},{9,10},{10,1... | collective-permute-start | bytes 2211848 | tf_op jit(solution)/shard_map/ppermute | solution.py:92
  35.3 0.9 collective-permute-start.7
  36.2 1.4 collective-permute-start.8
  37.6 1.3 collective-permute-start.9
  39.6 15.7 %shard_map.71 = (f32[256,256]{1,0:T(8,128)}, f32[256,384]{1,0:T(8,128)}) custom-call(s32[1,384]{1,0:T(1,128)} %sub.28.slot_abs_ref, s32[1,384]{1,0:T(1,128)} %reshape.189.slot_rel_ref, f32[384,256]{1,0:T(8,128)} %bitcast.17), custom_call_target="tpu_custom_call" | custom-call | tf_op jit(solution)/shard_map/pallas_call | solution.py:207
  55.4 0.8 copy-done
  56.9 2.4 %shard_map.73 = (f32[48,1920]{1,0:T(8,128)}, f32[48,1920]{1,0:T(8,128)}, f32[48,1920]{1,0:T(8,128)}, f32[48,1920]{1,0:T(8,128)}) custom-call(f32[96,1920]{1,0:T(8,128)} %copy-done, f32[96,1920]{1,0:T(8,128)} %copy-done.1, f32[96,1920]{1,0:T(8,128)} %copy-done.2, f32[96,1920]{1,0:T(8,128)} %copy-done.3), custom_call_target="tpu_custom_call" | custom-call | tf_op jit(solution)/shard_map/pallas_call | solution.py:118
  60.0 2.1 %collective-permute-start.11 = (f32[48,1920]{1,0:T(8,128)}, f32[48,1920]{1,0:T(8,128)S(1)}, u32[]{:S(2)}, u32[]{:S(2)}) collective-permute-start(f32[48,1920]{1,0:T(8,128)} %get-tuple-element.63), channel_id=1, source_target_pairs={{0,3},{1,0},{2,1},{3,2},{4,7},{5,4},{6,5},{7,6},{8,11},{9,8},{10,9... | collective-permute-start | bytes 1105928 | tf_op jit(solution)/shard_map/ppermute | solution.py:92
  62.2 2.5 %collective-permute-start.13 = (f32[48,1920]{1,0:T(8,128)}, f32[48,1920]{1,0:T(8,128)S(1)}, u32[]{:S(2)}, u32[]{:S(2)}) collective-permute-start(f32[48,1920]{1,0:T(8,128)} %get-tuple-element.65), channel_id=1, source_target_pairs={{0,12},{1,13},{2,14},{3,15},{4,0},{5,1},{6,2},{7,3},{8,4},{9,5},{1... | collective-permute-start | bytes 1105928 | tf_op jit(solution)/shard_map/ppermute | solution.py:92
  64.7 0.8 copy.18.active_ref
  66.3 2.6 %shard_map.72 = (f32[256,256]{1,0:T(8,128)}, bf16[256,1152]{1,0:T(8,128)(2,1)}) custom-call(s32[256,1]{1,0:T(8,128)} %copy.18.active_ref, f32[256,256]{1,0:T(8,128)} %get-tuple-element.53.inv_ref, f32[256,384]{1,0:T(8,128)} %get-tuple-element.54.inv_rel_ref, f32[256,4096]{1,0:T(8,128)} %bitcast.15), custom_call_target="tpu_custom_call" | custom-call | tf_op jit(solution)/shard_map/pallas_call | solution.py:235
  68.9 1.2 collective-permute-done.12.refs_8_
  71.0 30.4 %shard_map.74 = (f32[256,4096]{1,0:T(8,128)}, f32[128,2,3840]{2,1,0:T(2,128)}) custom-call(s32[1,256]{1,0:T(1,128)} %bitcast.19, f32[256,256]{1,0:T(8,128)} %get-tuple-element.55.first_ref, bf16[256,1152]{1,0:T(8,128)(2,1)} %get-tuple-element.56.lower_ref, s32[3840,128]{1,0:T(8,128)} %shard_map.69.rank_hbm, f32[256,4096]{1,0:T(8,128)} %bitcast.16, ...), custom_call_target="tpu_custom_call" | custom-call | tf_op jit(solution)/shard_map/pallas_call | solution.py:372
  101.4 12.3 %all-to-all-start.1 = ((f32[128,2,3840]{2,1,0:T(2,128)}), f32[128,2,3840]{2,1,0:T(2,128)}, u32[]{:S(2)}, u32[]{:S(2)}) async-start(f32[128,2,3840]{2,1,0:T(2,128)} %get-tuple-element.67), calls=%async_computation.1 | async-start | bytes 7864320 | tf_op jit(solution)/shard_map/all_to_all | solution.py:534
  113.7 1.0 select_reduce_fusion.1
  114.7 1.3 select_reduce_fusion
  117.2 6.5 %fusion.21 = (bf16[8,64]{1,0:T(8,128)(2,1)S(1)}, f32[8,64,128]{2,1,0:T(8,128)S(1)}) fusion(s32[8,3840]{1,0:T(8,128)S(1)} %get-tuple-element.99, s32[8,3840]{1,0:T(8,128)S(1)} %get-tuple-element.98), kind=kOutput, calls=%fused_computation.74 | convolution fusion | flops 509279744 | bytes 508928 | tf_op jit(solution)/shard_map/fah,fal->fhl/dot_general | solution.py:453
  124.7 0.9 copy.21
  126.2 37.1 %all-to-all-done.1.received_ref = f32[128,2,3840]{2,1,0:T(2,128)} async-done(((f32[128,2,3840]{2,1,0:T(2,128)}), f32[128,2,3840]{2,1,0:T(2,128)}, u32[]{:S(2)}, u32[]{:S(2)}) %all-to-all-start.1) | async-done | bytes 3932192 | tf_op jit(solution)/shard_map/all_to_all | solution.py:534
  163.3 11.7 %shard_map.75 = f32[64,8192]{1,0:T(8,128)} custom-call(s32[8,64]{1,0:T(8,128)} %fusion.13.group_ref, s32[8,8192]{1,0:T(8,128)} %bitcast.18, bf16[64,256]{1,0:T(8,128)(2,1)} %convert_element_type.45.put_ref, f32[128,2,3840]{2,1,0:T(2,128)} %all-to-all-done.1.received_ref, f32[64,8192]{1,0:T(8,128)} %parent_ref.1), custom_call_target="tpu_custom_call" | custom-call | tf_op jit(solution)/shard_map/pallas_call | solution.py:430
  (90 shorter events, 10.7 us)
Async XLA Ops:
  0.6 17.8 %copy-start.18 = (s32[4]{0:T(128)S(1)}, s32[4]{0:T(128)}, u32[]{:S(2)}) copy-start(s32[4]{0:T(128)} %constant.137.clone) | copy-start | bytes 52
  0.6 23.0 %copy-start.5 = (s32[8,3840]{1,0:T(8,128)S(1)}, s32[8,3840]{1,0:T(8,128)}, u32[]{:S(2)}) copy-start(s32[8,3840]{1,0:T(8,128)} %param.7) | copy-start | bytes 368644
  2.3 36.6 %copy-start.17 = (s32[1,256]{1,0:T(1,128)S(1)}, s32[1,256]{1,0:T(1,128)}, u32[]{:S(2)}) copy-start(s32[1,256]{1,0:T(1,128)} %get-tuple-element.95.ids_ref) | copy-start | bytes 3076
  6.4 13.5 %collective-permute-start = (f32[24,1920]{1,0:T(8,128)}, f32[24,1920]{1,0:T(8,128)S(1)}, u32[]{:S(2)}, u32[]{:S(2)}) collective-permute-start(f32[24,1920]{1,0:T(8,128)} %get-tuple-element.38.refs_0_), channel_id=1, source_target_pairs={{0,4},{1,5},{2,6},{3,7},{4,8},{5,9},{6,10},{7,11},{8,12},{9,13},{1... | collective-permute-start | bytes 552968 | tf_op jit(solution)/shard_map/ppermute | solution.py:92
  8.4 19.8 %collective-permute-start.1 = (f32[24,1920]{1,0:T(8,128)}, f32[24,1920]{1,0:T(8,128)S(1)}, u32[]{:S(2)}, u32[]{:S(2)}) collective-permute-start(f32[24,1920]{1,0:T(8,128)} %get-tuple-element.38.refs_0_), channel_id=1, source_target_pairs={{0,12},{1,13},{2,14},{3,15},{4,0},{5,1},{6,2},{7,3},{8,4},{9,5},{1... | collective-permute-start | bytes 552968 | tf_op jit(solution)/shard_map/ppermute | solution.py:92
  9.7 18.5 %collective-permute-start.2 = (f32[24,1920]{1,0:T(8,128)}, f32[24,1920]{1,0:T(8,128)S(1)}, u32[]{:S(2)}, u32[]{:S(2)}) collective-permute-start(f32[24,1920]{1,0:T(8,128)} %get-tuple-element.38.refs_0_), channel_id=1, source_target_pairs={{0,8},{1,9},{2,10},{3,11},{4,12},{5,13},{6,14},{7,15},{8,0},{9,1},... | collective-permute-start | bytes 552968 | tf_op jit(solution)/shard_map/ppermute | solution.py:92
  11.4 16.8 %collective-permute-start.3 = (f32[24,1920]{1,0:T(8,128)}, f32[24,1920]{1,0:T(8,128)S(1)}, u32[]{:S(2)}, u32[]{:S(2)}) collective-permute-start(f32[24,1920]{1,0:T(8,128)} %get-tuple-element.42.refs_4_), channel_id=1, source_target_pairs={{0,1},{1,2},{2,3},{3,0},{4,5},{5,6},{6,7},{7,4},{8,9},{9,10},{10,1... | collective-permute-start | bytes 552968 | tf_op jit(solution)/shard_map/ppermute | solution.py:92
  12.7 15.5 %collective-permute-start.4 = (f32[24,1920]{1,0:T(8,128)}, f32[24,1920]{1,0:T(8,128)S(1)}, u32[]{:S(2)}, u32[]{:S(2)}) collective-permute-start(f32[24,1920]{1,0:T(8,128)} %get-tuple-element.42.refs_4_), channel_id=1, source_target_pairs={{0,3},{1,0},{2,1},{3,2},{4,7},{5,4},{6,5},{7,6},{8,11},{9,8},{10,9... | collective-permute-start | bytes 552968 | tf_op jit(solution)/shard_map/ppermute | solution.py:92
  14.2 16.1 %all-to-all-start = ((f32[16,24,256]{2,1,0:T(8,128)}), f32[16,24,256]{2,1,0:T(8,128)S(1)}, u32[]{:S(2)}, u32[]{:S(2)}) async-start(f32[16,24,256]{2,1,0:T(8,128)} %get-tuple-element.37), calls=%async_computation | async-start | bytes 786432 | tf_op jit(solution)/shard_map/all_to_all | solution.py:487
  19.9 10.4 %copy-start.10 = (f32[24,1920]{1,0:T(8,128)}, f32[24,1920]{1,0:T(8,128)S(1)}, u32[]{:S(2)}) copy-start(f32[24,1920]{1,0:T(8,128)S(1)} %collective-permute-done.refs_1_) | copy-start | bytes 552964
  19.9 10.4 %collective-permute-start.5 = (f32[24,1920]{1,0:T(8,128)}, f32[24,1920]{1,0:T(8,128)S(1)}, u32[]{:S(2)}, u32[]{:S(2)}) collective-permute-start(f32[24,1920]{1,0:T(8,128)} %get-tuple-element.42.refs_4_), channel_id=1, source_target_pairs={{0,2},{1,3},{2,0},{3,1},{4,6},{5,7},{6,4},{7,5},{8,10},{9,11},{10,... | collective-permute-start | bytes 552968 | tf_op jit(solution)/shard_map/ppermute | solution.py:92
  28.2 2.1 %copy-start.11 = (f32[24,1920]{1,0:T(8,128)}, f32[24,1920]{1,0:T(8,128)S(1)}, u32[]{:S(2)}) copy-start(f32[24,1920]{1,0:T(8,128)S(1)} %collective-permute-done.1.refs_2_) | copy-start | bytes 552964
  28.2 2.1 %copy-start.12 = (f32[24,1920]{1,0:T(8,128)}, f32[24,1920]{1,0:T(8,128)S(1)}, u32[]{:S(2)}) copy-start(f32[24,1920]{1,0:T(8,128)S(1)} %collective-permute-done.2.refs_3_) | copy-start | bytes 552964
  28.2 2.1 %copy-start.13 = (f32[24,1920]{1,0:T(8,128)}, f32[24,1920]{1,0:T(8,128)S(1)}, u32[]{:S(2)}) copy-start(f32[24,1920]{1,0:T(8,128)S(1)} %collective-permute-done.3.refs_5_) | copy-start | bytes 552964
  28.2 2.1 %copy-start.14 = (f32[24,1920]{1,0:T(8,128)}, f32[24,1920]{1,0:T(8,128)S(1)}, u32[]{:S(2)}) copy-start(f32[24,1920]{1,0:T(8,128)S(1)} %collective-permute-done.4.refs_6_) | copy-start | bytes 552964
  30.3 9.3 %copy-start.4 = (f32[16,24,256]{2,1,0:T(8,128)}, f32[16,24,256]{2,1,0:T(8,128)S(1)}, u32[]{:S(2)}) copy-start(f32[16,24,256]{2,1,0:T(8,128)S(1)} %all-to-all-done) | copy-start | bytes 1179652
  33.5 21.8 %collective-permute-start.6 = (f32[96,1920]{1,0:T(8,128)}, f32[96,1920]{1,0:T(8,128)S(1)}, u32[]{:S(2)}, u32[]{:S(2)}) collective-permute-start(f32[96,1920]{1,0:T(8,128)} %get-tuple-element.46.refs_0_), channel_id=1, source_target_pairs={{0,1},{1,2},{2,3},{3,0},{4,5},{5,6},{6,7},{7,4},{8,9},{9,10},{10,1... | collective-permute-start | bytes 2211848 | tf_op jit(solution)/shard_map/ppermute | solution.py:92
  35.3 20.0 %collective-permute-start.7 = (f32[96,1920]{1,0:T(8,128)}, f32[96,1920]{1,0:T(8,128)S(1)}, u32[]{:S(2)}, u32[]{:S(2)}) collective-permute-start(f32[96,1920]{1,0:T(8,128)} %get-tuple-element.46.refs_0_), channel_id=1, source_target_pairs={{0,3},{1,0},{2,1},{3,2},{4,7},{5,4},{6,5},{7,6},{8,11},{9,8},{10,9... | collective-permute-start | bytes 2211848 | tf_op jit(solution)/shard_map/ppermute | solution.py:92
  36.2 19.1 %collective-permute-start.8 = (f32[96,1920]{1,0:T(8,128)}, f32[96,1920]{1,0:T(8,128)S(1)}, u32[]{:S(2)}, u32[]{:S(2)}) collective-permute-start(f32[96,1920]{1,0:T(8,128)} %get-tuple-element.47.refs_5_), channel_id=1, source_target_pairs={{0,4},{1,5},{2,6},{3,7},{4,8},{5,9},{6,10},{7,11},{8,12},{9,13},{1... | collective-permute-start | bytes 2211848 | tf_op jit(solution)/shard_map/ppermute | solution.py:92
  37.6 17.8 %collective-permute-start.9 = (f32[96,1920]{1,0:T(8,128)}, f32[96,1920]{1,0:T(8,128)S(1)}, u32[]{:S(2)}, u32[]{:S(2)}) collective-permute-start(f32[96,1920]{1,0:T(8,128)} %get-tuple-element.47.refs_5_), channel_id=1, source_target_pairs={{0,12},{1,13},{2,14},{3,15},{4,0},{5,1},{6,2},{7,3},{8,4},{9,5},{1... | collective-permute-start | bytes 2211848 | tf_op jit(solution)/shard_map/ppermute | solution.py:92
  55.3 0.9 copy-start
  55.3 1.1 copy-start.1
  55.3 1.3 copy-start.2
  55.4 1.6 copy-start.3
  59.4 9.5 %collective-permute-start.10 = (f32[48,1920]{1,0:T(8,128)}, f32[48,1920]{1,0:T(8,128)S(1)}, u32[]{:S(2)}, u32[]{:S(2)}) collective-permute-start(f32[48,1920]{1,0:T(8,128)} %get-tuple-element.62), channel_id=1, source_target_pairs={{0,1},{1,2},{2,3},{3,0},{4,5},{5,6},{6,7},{7,4},{8,9},{9,10},{10,1... | collective-permute-start | bytes 1105928 | tf_op jit(solution)/shard_map/ppermute | solution.py:92
  60.0 8.9 %collective-permute-start.11 = (f32[48,1920]{1,0:T(8,128)}, f32[48,1920]{1,0:T(8,128)S(1)}, u32[]{:S(2)}, u32[]{:S(2)}) collective-permute-start(f32[48,1920]{1,0:T(8,128)} %get-tuple-element.63), channel_id=1, source_target_pairs={{0,3},{1,0},{2,1},{3,2},{4,7},{5,4},{6,5},{7,6},{8,11},{9,8},{10,9... | collective-permute-start | bytes 1105928 | tf_op jit(solution)/shard_map/ppermute | solution.py:92
  62.0 8.1 %collective-permute-start.12 = (f32[48,1920]{1,0:T(8,128)}, f32[48,1920]{1,0:T(8,128)S(1)}, u32[]{:S(2)}, u32[]{:S(2)}) collective-permute-start(f32[48,1920]{1,0:T(8,128)} %get-tuple-element.64), channel_id=1, source_target_pairs={{0,4},{1,5},{2,6},{3,7},{4,8},{5,9},{6,10},{7,11},{8,12},{9,13},{1... | collective-permute-start | bytes 1105928 | tf_op jit(solution)/shard_map/ppermute | solution.py:92
  62.2 7.9 %collective-permute-start.13 = (f32[48,1920]{1,0:T(8,128)}, f32[48,1920]{1,0:T(8,128)S(1)}, u32[]{:S(2)}, u32[]{:S(2)}) collective-permute-start(f32[48,1920]{1,0:T(8,128)} %get-tuple-element.65), channel_id=1, source_target_pairs={{0,12},{1,13},{2,14},{3,15},{4,0},{5,1},{6,2},{7,3},{8,4},{9,5},{1... | collective-permute-start | bytes 1105928 | tf_op jit(solution)/shard_map/ppermute | solution.py:92
  68.9 1.3 copy-start.6
  68.9 1.3 copy-start.7
  101.4 13.3 %copy-start.16 = (s32[8,4096]{1,0:T(8,128)S(1)}, s32[8,4096]{1,0:T(8,128)}, u32[]{:S(2)}) copy-start(s32[8,4096]{1,0:T(8,128)} %param.6) | copy-start | bytes 393220
  101.4 61.9 %all-to-all-start.1 = ((f32[128,2,3840]{2,1,0:T(2,128)}), f32[128,2,3840]{2,1,0:T(2,128)}, u32[]{:S(2)}, u32[]{:S(2)}) async-start(f32[128,2,3840]{2,1,0:T(2,128)} %get-tuple-element.67), calls=%async_computation.1 | async-start | bytes 7864320 | tf_op jit(solution)/shard_map/all_to_all | solution.py:534
  (3 other events, 2.3 us)
